TPU v7x, 256 devices: a whole 4x4x8 slice. The times are simulated.
256 devices in a mesh: tile: 64 (over y, x_lo, z), src: 4 (over x_hi, core).
Axes of the slice: x: 4 (x_hi: 2, x_lo: 2; x = x_hi * 2 + x_lo), y: 4, z: 8, core: 2. Of those that a mesh axis runs over, the one named last changes fastest.
Arguments:
- excitation: bfloat16 [2, 512, 65536], P(None, 'src', 'tile'), may hold values from -6 to 6
- near_blocks: bfloat16 [128, 3, 2, 512, 512], P('tile'), may hold values from -0.02734375 to 0.02734375
- source_basis: bfloat16 [128, 2, 24, 512], P('tile'), may hold values from -0.1875 to 0.1875
- target_basis: bfloat16 [128, 2, 24, 512], P('tile'), may hold values from -0.625 to 0.625
- coupling: bfloat16 [2, 3072, 3072], P(None, None, 'tile'), may hold values from -0.0390625 to 0.0390625
- pair_rank: int32 [128, 128], P(None, 'tile'), may hold values from 2 to 24
- far_link: int32 [128, 128], P(None, 'tile'), may hold values 0 or 1
- focal_kernel: bfloat16 [2, 512, 65536], P(None, None, 'tile'), may hold values from -0.015625 to 0.015625
- focal_target: float32 [512], replicated, may hold values from 0.3 to 0.9
- focal_owner: int32 [512], replicated, may hold values from 0 to 511, each once
Outputs:
- field: float32 [2, 512, 65536], P(None, 'src', 'tile')
- focal_residual: float32 [512], P('tile')
- adjoint: float32 [2, 512, 65536], P(None, 'src', 'tile')
Inputs may be any that keep to these rules, and one draw needn't show every extreme that they name: `focal_owner`: each focal point has its own slot; slot k belongs to index k // 8 of tile.
All inputs are finite; a program needn't handle non-finite values. No bound on the sum of `far_link` on one device may be relied on, other than what follows from the above.
Results may differ from a plain program's by a relative error of at most 0.006.
Values may be sent and summed in bfloat16 or wider, within the bound.
A program may use at most 64 MiB of HBM per device.

v0:
```python
import jax
import jax.numpy as jnp
from jax import lax
from jax.sharding import PartitionSpec as P

TILE = 512
RANK = 24


DAMPING = 0.8


def extended(x, sides, width):
    for axis, dim in sides:
        size, length = (lax.axis_size(axis), x.shape[dim])
        up = [(i, (i + 1) % size) for i in range(size)]
        down = [(j, i) for i, j in up]
        last = lax.slice_in_dim(x, length - width, length, axis=dim)
        initial = lax.slice_in_dim(x, 0, width, axis=dim)
        before = lax.ppermute(last, axis, up)
        after = lax.ppermute(initial, axis, down)
        x = jnp.concatenate([before, x, after], axis=dim)
    return x


def laid_out(blocks, dim):
    dims = list(blocks.shape[1:])
    dims[dim] *= blocks.shape[0]
    return jnp.moveaxis(blocks, 0, dim).reshape(dims)


def from_everyone(x, axis):
    length = lax.axis_size(axis)
    return lax.all_to_all(jnp.broadcast_to(x[None], (length, *x.shape)), axis, 0, 0, tiled=True)


def collect(x, axis, dim):
    return laid_out(from_everyone(x, axis), dim)


def split_up(x, dim, length):
    dims = x.shape
    blocks = x.reshape(*dims[:dim], length, dims[dim] // length, *dims[dim + 1 :])
    return jnp.moveaxis(blocks, dim, 0)


def sum_at_owner(x, axis, dim):
    length = lax.axis_size(axis)
    blocks = lax.all_to_all(split_up(x, dim, length), axis, 0, 0, tiled=True)
    return jnp.sum(blocks, axis=0)


def taken_together(x, axis):
    return from_everyone(x, axis).sum(axis=0)


def plain_dot(left, right, contract):
    return lax.dot_general(
        left, right, (((1,), (contract,)), ((), ())), preferred_element_type=jnp.float32
    )


def complex_dot(left_re, left_im, right_re, right_im, contract):
    real_part = plain_dot(left_re, right_re, contract) - plain_dot(left_im, right_im, contract)
    imag_part = plain_dot(left_re, right_im, contract) + plain_dot(left_im, right_re, contract)
    return (real_part, imag_part)


def per_device(
    excitation,
    near_blocks,
    source_basis,
    target_basis,
    coupling,
    pair_rank,
    far_link,
    focal_kernel,
    focal_target,
    focal_owner,
):
    tile_count = near_blocks.shape[0]
    src_rows = excitation.shape[1]
    tiles = pair_rank.shape[0]
    focal_count = focal_target.shape[0]
    first_tile = lax.axis_index("tile") * tile_count
    global_tiles = first_tile + jnp.arange(tile_count)
    source_tiles = jnp.arange(tiles)[:, None]
    distance = (global_tiles[None, :] - source_tiles) % tiles
    far_pairs = (far_link == 1) & (distance != 0) & (distance != 1) & (distance != tiles - 1)
    levels = jnp.arange(RANK)
    rank_limit = pair_rank[:, None, :, None]
    rank_mask = (
        far_pairs[:, None, :, None]
        & (levels[None, :, None, None] < rank_limit)
        & (levels[None, None, None, :] < rank_limit)
    )
    rank_mask = rank_mask.reshape(tiles * RANK, tile_count * RANK)
    masked = coupling * rank_mask.astype(coupling.dtype)
    flipped = lax.all_to_all(masked, "tile", split_axis=1, concat_axis=2, tiled=True)

    def apply_transpose(field):
        field_bf = field.astype(jnp.bfloat16)
        moved_re = [[], [], []]
        moved_im = [[], [], []]
        proj_re = []
        proj_im = []
        for tile_here in range(tile_count):
            own = field_bf[:, :, tile_here * TILE : (tile_here + 1) * TILE]
            for offset in range(3):
                part_re, part_im = complex_dot(
                    own[0],
                    own[1],
                    near_blocks[tile_here, offset, 0],
                    near_blocks[tile_here, offset, 1],
                    1,
                )
                moved_re[offset].append(part_re)
                moved_im[offset].append(part_im)
            part_re, part_im = complex_dot(
                own[0], own[1], target_basis[tile_here, 0], target_basis[tile_here, 1], 1
            )
            proj_re.append(part_re)
            proj_im.append(part_im)
        moved = [
            jnp.stack([jnp.concatenate(moved_re[k], axis=1), jnp.concatenate(moved_im[k], axis=1)])
            for k in range(3)
        ]
        width = tile_count * TILE
        edges = jnp.concatenate([moved[0][:, :, 0:TILE], moved[2][:, :, width - TILE :]], axis=2)
        arrived = extended(edges.astype(jnp.bfloat16), (("tile", 2),), TILE).astype(edges.dtype)
        from_left = jnp.concatenate(
            [arrived[:, :, 0:TILE], moved[2][:, :, 0 : width - TILE]], axis=2
        )
        from_right = jnp.concatenate(
            [moved[0][:, :, TILE:], arrived[:, :, 3 * TILE : 4 * TILE]], axis=2
        )
        near_part = moved[1] + from_left + from_right
        projected = jnp.stack(
            [jnp.concatenate(proj_re, axis=1), jnp.concatenate(proj_im, axis=1)]
        ).astype(jnp.bfloat16)
        shard_piece = collect(projected, "tile", 2)
        term_re, term_im = complex_dot(shard_piece[0], shard_piece[1], flipped[0], flipped[1], 1)
        summed_back = jnp.stack([term_re, term_im]).astype(jnp.bfloat16)
        far_re = []
        far_im = []
        for tile_here in range(tile_count):
            piece = summed_back[:, :, tile_here * RANK : (tile_here + 1) * RANK]
            part_re, part_im = complex_dot(
                piece[0], piece[1], source_basis[tile_here, 0], source_basis[tile_here, 1], 0
            )
            far_re.append(part_re)
            far_im.append(part_im)
        far_part = jnp.stack([jnp.concatenate(far_re, axis=1), jnp.concatenate(far_im, axis=1)])
        return field + near_part + far_part

    right_side = excitation.astype(jnp.float32)
    field = right_side
    for update in range(2):
        apply_field_bf = field.astype(jnp.bfloat16)
        padded = extended(apply_field_bf, (("tile", 2),), TILE)
        coeff_re = []
        coeff_im = []
        for apply_tile_here in range(tile_count):
            apply_own = apply_field_bf[:, :, apply_tile_here * TILE : (apply_tile_here + 1) * TILE]
            apply_part_re, apply_part_im = complex_dot(
                apply_own[0],
                apply_own[1],
                source_basis[apply_tile_here, 0],
                source_basis[apply_tile_here, 1],
                1,
            )
            coeff_re.append(apply_part_re)
            coeff_im.append(apply_part_im)
        coeff = jnp.stack(
            [jnp.concatenate(coeff_re, axis=1), jnp.concatenate(coeff_im, axis=1)]
        ).astype(jnp.bfloat16)
        fold_shard_piece = collect(coeff, "tile", 2)
        fold_term_re, fold_term_im = complex_dot(
            fold_shard_piece[0], fold_shard_piece[1], masked[0], masked[1], 0
        )
        coupled = jnp.stack([fold_term_re, fold_term_im]).astype(jnp.bfloat16)
        out_re = []
        out_im = []
        for apply_tile_here in range(tile_count):
            total_re = jnp.zeros((src_rows, TILE), jnp.float32)
            total_im = jnp.zeros((src_rows, TILE), jnp.float32)
            for apply_offset in range(3):
                window = padded[
                    :,
                    :,
                    (apply_tile_here + apply_offset)
                    * TILE : (apply_tile_here + apply_offset + 1)
                    * TILE,
                ]
                apply_part_re, apply_part_im = complex_dot(
                    window[0],
                    window[1],
                    near_blocks[apply_tile_here, apply_offset, 0],
                    near_blocks[apply_tile_here, apply_offset, 1],
                    0,
                )
                total_re = total_re + apply_part_re
                total_im = total_im + apply_part_im
            apply_piece = coupled[:, :, apply_tile_here * RANK : (apply_tile_here + 1) * RANK]
            apply_part_re, apply_part_im = complex_dot(
                apply_piece[0],
                apply_piece[1],
                target_basis[apply_tile_here, 0],
                target_basis[apply_tile_here, 1],
                0,
            )
            out_re.append(total_re + apply_part_re)
            out_im.append(total_im + apply_part_im)
        added = jnp.stack([jnp.concatenate(out_re, axis=1), jnp.concatenate(out_im, axis=1)])
        field = field + DAMPING * (right_side - (field + added))
    field_bf = field.astype(jnp.bfloat16)
    focal_re, focal_im = complex_dot(field_bf[0], field_bf[1], focal_kernel[0], focal_kernel[1], 1)
    slots_here = focal_count // lax.axis_size("tile")
    first_slot = lax.axis_index("tile") * slots_here
    sources = src_rows * lax.axis_size("src")
    permute = (focal_owner[:, None] == jnp.arange(focal_count)[None, :]).astype(jnp.float32)
    slotted = jnp.stack(
        [
            jnp.dot(focal_re, permute, precision=lax.Precision.HIGHEST),
            jnp.dot(focal_im, permute, precision=lax.Precision.HIGHEST),
        ]
    )
    owned_sums = sum_at_owner(slotted, "tile", 2)
    intensity = taken_together(
        jnp.sum(owned_sums[0] * owned_sums[0] + owned_sums[1] * owned_sums[1], axis=0), "src"
    )
    target_slots = jnp.dot(focal_target, permute, precision=lax.Precision.HIGHEST)
    target_part = lax.dynamic_slice_in_dim(target_slots, first_slot, slots_here)
    residual_out = jnp.tanh(intensity / (2.0 * sources)) - target_part
    slot_weights = jnp.stack([residual_out * owned_sums[0], -residual_out * owned_sums[1]]).astype(
        jnp.bfloat16
    )
    all_weights = collect(slot_weights, "tile", 2)
    permute_bf = permute.astype(jnp.bfloat16)
    weights_re = plain_dot(all_weights[0], permute_bf, 1).astype(jnp.bfloat16)
    weights_im = plain_dot(all_weights[1], permute_bf, 1).astype(jnp.bfloat16)
    scale_factor = (tiles * TILE / focal_count) ** 0.5
    term_re, term_im = complex_dot(weights_re, weights_im, focal_kernel[0], focal_kernel[1], 0)
    source_term = jnp.stack([term_re, term_im]) * scale_factor
    adjoint = source_term + DAMPING * (source_term - apply_transpose(source_term))
    return (field, residual_out, adjoint)


def solution(mesh):
    return jax.shard_map(
        per_device,
        mesh=mesh,
        in_specs=(
            P(None, "src", "tile"),
            P("tile", None, None, None, None),
            P("tile", None, None, None),
            P("tile", None, None, None),
            P(None, None, "tile"),
            P(None, "tile"),
            P(None, "tile"),
            P(None, None, "tile"),
            P(),
            P(),
        ),
        out_specs=(P(None, "src", "tile"), P("tile"), P(None, "src", "tile")),
        check_vma=False,
    )
```

profile of v0, /device:TPU:1, one launch (start us, length us, event | category | flops | bytes accessed | tf_op | source)
XLA Modules:
  0.0 324.6 jit_solution(974862746217765755)
XLA Ops:
  10.6 13.8 %all-to-all-start = ((bf16[64,2,128,48]{2,3,1,0:T(8,128)(2,1)}), bf16[64,2,128,48]{2,3,1,0:T(8,128)(2,1)}, u32[]{:S(2)}, u32[]{:S(2)}) async-start(bf16[64,2,128,48]{2,3,1,0:T(8,128)(2,1)} %broadcast_in_dim.10), calls=%async_computation | async-start | bytes 3145728 | tf_op jit(solution)/shard_map/all_to_all | solution.py:34
  26.2 5.2 %collective-permute-start.1 = (bf16[2,128,512]{2,1,0:T(8,128)(2,1)}, bf16[2,128,512]{2,1,0:T(8,128)(2,1)}, u32[]{:S(2)}, u32[]{:S(2)}) collective-permute-start(bf16[2,128,512]{2,1,0:T(8,128)(2,1)} %get-tuple-element.16), channel_id=1, source_target_pairs={{4,0},{8,4},{12,8},{16,12},{20,16},{24,20},{28,24},{32,28},{36,32}... | collective-permute-start | bytes 786440 | tf_op jit(solution)/shard_map/ppermute | solution.py:21
  39.4 2.0 convolution_subtract_fusion.16
  41.4 2.0 convolution_subtract_fusion.17
  43.4 2.0 convolution_subtract_fusion.14
  45.4 2.0 convolution_add_fusion.16
  49.8 3.0 reshape.190
  52.7 2.0 convolution_add_fusion.17
  56.0 2.1 fusion.3
  60.5 2.0 fusion.6
  62.5 6.8 %collective-permute-done = bf16[2,128,512]{2,1,0:T(8,128)(2,1)} collective-permute-done((bf16[2,128,512]{2,1,0:T(8,128)(2,1)}, bf16[2,128,512]{2,1,0:T(8,128)(2,1)}, u32[]{:S(2)}, u32[]{:S(2)}) %collective-permute-start) | collective-permute-done | bytes 262176 | tf_op jit(solution)/shard_map/ppermute | solution.py:20
  69.2 2.1 fusion.188
  71.3 2.1 fusion.196
  73.3 2.0 fusion.98
  75.4 2.1 fusion.106
  77.5 1.7 copy.70
  96.9 5.7 %all-to-all-start.1 = ((bf16[64,2,128,48]{2,3,1,0:T(8,128)(2,1)}), bf16[64,2,128,48]{2,3,1,0:T(8,128)(2,1)S(1)}, u32[]{:S(2)}, u32[]{:S(2)}) async-start(bf16[64,2,128,48]{2,3,1,0:T(8,128)(2,1)} %broadcast_in_dim.11), calls=%async_computation.1 | async-start | bytes 3145728 | tf_op jit(solution)/shard_map/all_to_all | solution.py:34
  104.9 4.8 %collective-permute-start.3 = (bf16[2,128,512]{2,1,0:T(8,128)(2,1)S(1)}, bf16[2,128,512]{2,1,0:T(8,128)(2,1)S(1)}, u32[]{:S(2)}, u32[]{:S(2)}) collective-permute-start(bf16[2,128,512]{2,1,0:T(8,128)(2,1)S(1)} %get-tuple-element.14), channel_id=1, source_target_pairs={{4,0},{8,4},{12,8},{16,12},{20,16},{24,20},{28,24},{32,28},{36,32}... | collective-permute-start | bytes 786440 | tf_op jit(solution)/shard_map/ppermute | solution.py:21
  109.7 2.1 convolution_subtract_fusion.10
  113.1 2.1 convolution_add_fusion.11
  115.2 2.0 convolution_add_fusion.10
  118.6 2.0 fusion.9
  121.8 2.0 fusion.12
  123.8 23.5 %collective-permute-done.2 = bf16[2,128,512]{2,1,0:T(8,128)(2,1)S(1)} collective-permute-done((bf16[2,128,512]{2,1,0:T(8,128)(2,1)S(1)}, bf16[2,128,512]{2,1,0:T(8,128)(2,1)S(1)}, u32[]{:S(2)}, u32[]{:S(2)}) %collective-permute-start.2) | collective-permute-done | bytes 262176 | tf_op jit(solution)/shard_map/ppermute | solution.py:20
  150.0 2.1 fusion.95
  152.1 2.0 fusion.103
  169.2 5.8 %all-to-all-start.2 = ((f32[64,2,128,8]{2,3,1,0:T(8,128)}), f32[64,2,128,8]{2,3,1,0:T(8,128)S(1)}, u32[]{:S(2)}, u32[]{:S(2)}) async-start(f32[64,2,128,8]{2,3,1,0:T(8,128)} %copy.53), calls=%async_computation.2 | async-start | bytes 1048576 | tf_op jit(solution)/shard_map/all_to_all | solution.py:49
  174.9 1.9 copy.57
  176.8 13.5 %all-to-all-done.2 = f32[64,2,128,8]{2,3,1,0:T(8,128)S(1)} async-done(((f32[64,2,128,8]{2,3,1,0:T(8,128)}), f32[64,2,128,8]{2,3,1,0:T(8,128)S(1)}, u32[]{:S(2)}, u32[]{:S(2)}) %all-to-all-start.2) | async-done | bytes 524320 | tf_op jit(solution)/shard_map/all_to_all | solution.py:49
  191.1 7.9 %all-to-all-start.3 = ((f32[4,1,8]{2,1,0:T(1,128)}), f32[4,1,8]{2,1,0:T(1,128)S(1)}, u32[]{:S(2)}, u32[]{:S(2)}) async-start(f32[4,1,8]{2,1,0:T(1,128)} %broadcast_in_dim.12), calls=%async_computation.3 | async-start | bytes 4096 | tf_op jit(solution)/shard_map/all_to_all | solution.py:34
  199.0 2.8 reshape.197
  201.8 1.6 all-to-all-done.3
  203.5 5.0 %all-to-all-start.6 = ((bf16[64,2,2304]{2,1,0:T(2,128)(2,1)}), bf16[64,2,2304]{2,1,0:T(2,128)(2,1)S(1)}, u32[]{:S(2)}, u32[]{:S(2)}) async-start(bf16[64,2,2304]{2,1,0:T(2,128)(2,1)} %reshape.197), calls=%async_computation.6 | async-start | bytes 1179648 | tf_op jit(solution)/shard_map/all_to_all | solution.py:99
  209.1 15.9 %all-to-all-done.6 = bf16[64,2,2304]{2,1,0:T(2,128)(2,1)S(1)} async-done(((bf16[64,2,2304]{2,1,0:T(2,128)(2,1)}), bf16[64,2,2304]{2,1,0:T(2,128)(2,1)S(1)}, u32[]{:S(2)}, u32[]{:S(2)}) %all-to-all-start.6) | async-done | bytes 589856 | tf_op jit(solution)/shard_map/all_to_all | solution.py:99
  225.8 7.4 %all-to-all-start.4 = ((bf16[64,2,128,8]{2,3,1,0:T(8,128)(2,1)}), bf16[64,2,128,8]{2,3,1,0:T(8,128)(2,1)S(1)}, u32[]{:S(2)}, u32[]{:S(2)}) async-start(bf16[64,2,128,8]{2,3,1,0:T(8,128)(2,1)} %broadcast_in_dim.13), calls=%async_computation.4 | async-start | bytes 524288 | tf_op jit(solution)/shard_map/all_to_all | solution.py:34
  233.2 2.6 reshape.198
  235.8 5.5 %copy.59 = bf16[2,64,48,48]{1,2,3,0:T(8,128)(2,1)} copy(bf16[2,64,48,48]{3,0,2,1:T(2,128)(2,1)} %bitcast.662) | data formatting | bytes 1179648 | tf_op jit(solution)/shard_map/all_to_all | solution.py:99
  241.3 2.9 all-to-all-done.4
  245.1 1.5 fusion.71
  246.6 1.7 fusion.64
  248.3 1.5 fusion
  260.0 8.1 %all-to-all-start.5 = ((bf16[64,2,128,48]{2,3,1,0:T(8,128)(2,1)}), bf16[64,2,128,48]{2,3,1,0:T(8,128)(2,1)}, u32[]{:S(2)}, u32[]{:S(2)}) async-start(bf16[64,2,128,48]{2,3,1,0:T(8,128)(2,1)} %broadcast_in_dim.14), calls=%async_computation.5 | async-start | bytes 3145728 | tf_op jit(solution)/shard_map/all_to_all | solution.py:34
  269.7 1.6 convolution_subtract_fusion.3
  278.1 5.1 %collective-permute-start.5 = (bf16[2,128,512]{2,1,0:T(8,128)(2,1)S(1)}, bf16[2,128,512]{2,1,0:T(8,128)(2,1)S(1)}, u32[]{:S(2)}, u32[]{:S(2)}) collective-permute-start(bf16[2,128,512]{2,1,0:T(8,128)(2,1)S(1)} %fusion.88), channel_id=1, source_target_pairs={{4,0},{8,4},{12,8},{16,12},{20,16},{24,20},{28,24},{32,28},{36,32}... | collective-permute-start | bytes 786440 | tf_op jit(solution)/shard_map/ppermute | solution.py:21
  285.8 26.4 %collective-permute-done.4 = bf16[2,128,512]{2,1,0:T(8,128)(2,1)S(1)} collective-permute-done((bf16[2,128,512]{2,1,0:T(8,128)(2,1)S(1)}, bf16[2,128,512]{2,1,0:T(8,128)(2,1)S(1)}, u32[]{:S(2)}, u32[]{:S(2)}) %collective-permute-start.4) | collective-permute-done | bytes 262176 | tf_op jit(solution)/shard_map/ppermute | solution.py:20
  313.2 2.0 copy.68
  315.2 1.5 convolution_bitcast_fusion.2
  322.8 1.6 fusion.61
  (303 shorter events, 97.1 us)
Async XLA Ops:
  0.6 207.8 %copy-start = (f32[512]{0:T(512)S(1)}, f32[512]{0:T(512)}, u32[]{:S(2)}) copy-start(f32[512]{0:T(512)} %param.18) | copy-start | bytes 6148
  0.6 23.8 %copy-start.1 = (bf16[2,128,1024]{2,1,0:T(8,128)(2,1)S(1)}, bf16[2,128,1024]{2,1,0:T(8,128)(2,1)}, u32[]{:S(2)}) copy-start(bf16[2,128,1024]{2,1,0:T(8,128)(2,1)} %param.10) | copy-start | bytes 1572868
  2.8 36.3 %copy-start.50 = (s32[128,2]{0,1:T(2,128)S(1)}, s32[128,2]{0,1:T(2,128)}, u32[]{:S(2)}) copy-start(s32[128,2]{0,1:T(2,128)} %param.15) | copy-start | bytes 3076
  2.8 36.4 %copy-start.52 = (s32[128,2]{0,1:T(2,128)S(1)}, s32[128,2]{0,1:T(2,128)}, u32[]{:S(2)}) copy-start(s32[128,2]{0,1:T(2,128)} %param.16) | copy-start | bytes 3076
  10.6 66.8 %all-to-all-start = ((bf16[64,2,128,48]{2,3,1,0:T(8,128)(2,1)}), bf16[64,2,128,48]{2,3,1,0:T(8,128)(2,1)}, u32[]{:S(2)}, u32[]{:S(2)}) async-start(bf16[64,2,128,48]{2,3,1,0:T(8,128)(2,1)} %broadcast_in_dim.10), calls=%async_computation | async-start | bytes 3145728 | tf_op jit(solution)/shard_map/all_to_all | solution.py:34
  25.3 43.9 %collective-permute-start = (bf16[2,128,512]{2,1,0:T(8,128)(2,1)}, bf16[2,128,512]{2,1,0:T(8,128)(2,1)}, u32[]{:S(2)}, u32[]{:S(2)}) collective-permute-start(bf16[2,128,512]{2,1,0:T(8,128)(2,1)} %get-tuple-element.15), channel_id=1, source_target_pairs={{0,4},{4,8},{8,12},{12,16},{16,20},{20,24},{24,28},{28,32},{32,36}... | collective-permute-start | bytes 786440 | tf_op jit(solution)/shard_map/ppermute | solution.py:20
  26.2 47.1 %collective-permute-start.1 = (bf16[2,128,512]{2,1,0:T(8,128)(2,1)}, bf16[2,128,512]{2,1,0:T(8,128)(2,1)}, u32[]{:S(2)}, u32[]{:S(2)}) collective-permute-start(bf16[2,128,512]{2,1,0:T(8,128)(2,1)} %get-tuple-element.16), channel_id=1, source_target_pairs={{4,0},{8,4},{12,8},{16,12},{20,16},{24,20},{28,24},{32,28},{36,32}... | collective-permute-start | bytes 786440 | tf_op jit(solution)/shard_map/ppermute | solution.py:21
  71.3 8.9 %copy-start.21 = (bf16[2,2,24,512]{3,2,1,0:T(8,128)(2,1)S(1)}, bf16[2,2,24,512]{3,2,1,0:T(8,128)(2,1)}, u32[]{:S(2)}) copy-start(bf16[2,2,24,512]{3,2,1,0:T(8,128)(2,1)} %param.13) | copy-start | bytes 294916
  79.8 6.1 %copy-start.22 = (f32[128,512]{1,0:T(8,128)S(1)}, f32[128,512]{1,0:T(8,128)}, u32[]{:S(2)}) copy-start(f32[128,512]{1,0:T(8,128)} %fusion.196) | copy-start | bytes 786436
  79.8 6.1 %copy-start.25 = (f32[128,512]{1,0:T(8,128)S(1)}, f32[128,512]{1,0:T(8,128)}, u32[]{:S(2)}) copy-start(f32[128,512]{1,0:T(8,128)} %convolution_add_fusion.16) | copy-start | bytes 786436
  82.2 6.4 %copy-start.48 = (bf16[2,2,24,512]{3,2,1,0:T(8,128)(2,1)S(1)}, bf16[2,2,24,512]{3,2,1,0:T(8,128)(2,1)}, u32[]{:S(2)}) copy-start(bf16[2,2,24,512]{3,2,1,0:T(8,128)(2,1)} %param.12) | copy-start | bytes 294916
  84.7 8.4 %copy-start.16 = (f32[1,128,1024]{2,1,0:T(8,128)}, f32[1,128,1024]{2,1,0:T(8,128)S(1)}, u32[]{:S(2)}) copy-start(f32[1,128,1024]{2,1,0:T(8,128)S(1)} %maximum_bitcast_fusion) | copy-start | bytes 1572868
  87.2 8.3 %copy-start.18 = (f32[1,128,1024]{2,1,0:T(8,128)}, f32[1,128,1024]{2,1,0:T(8,128)S(1)}, u32[]{:S(2)}) copy-start(f32[1,128,1024]{2,1,0:T(8,128)S(1)} %maximum_bitcast_fusion.1) | copy-start | bytes 1572868
  87.4 7.9 %copy-start.2 = (bf16[2,128,1024]{2,1,0:T(8,128)(2,1)}, bf16[2,128,1024]{2,1,0:T(8,128)(2,1)S(1)}, u32[]{:S(2)}) copy-start(bf16[2,128,1024]{2,1,0:T(8,128)(2,1)S(1)} %fusion.86) | copy-start | bytes 1572868
  95.5 16.3 %copy-start.3 = (bf16[2,128,1024]{2,1,0:T(8,128)(2,1)S(1)}, bf16[2,128,1024]{2,1,0:T(8,128)(2,1)}, u32[]{:S(2)}) copy-start(bf16[2,128,1024]{2,1,0:T(8,128)(2,1)} %copy-done.2) | copy-start | bytes 1572868
  96.9 57.2 %all-to-all-start.1 = ((bf16[64,2,128,48]{2,3,1,0:T(8,128)(2,1)}), bf16[64,2,128,48]{2,3,1,0:T(8,128)(2,1)S(1)}, u32[]{:S(2)}, u32[]{:S(2)}) async-start(bf16[64,2,128,48]{2,3,1,0:T(8,128)(2,1)} %broadcast_in_dim.11), calls=%async_computation.1 | async-start | bytes 3145728 | tf_op jit(solution)/shard_map/all_to_all | solution.py:34
  102.6 15.9 %copy-start.32 = (f32[128,512]{1,0:T(8,128)S(1)}, f32[128,512]{1,0:T(8,128)}, u32[]{:S(2)}) copy-start(f32[128,512]{1,0:T(8,128)} %fusion.140) | copy-start | bytes 786436
  103.8 43.6 %collective-permute-start.2 = (bf16[2,128,512]{2,1,0:T(8,128)(2,1)S(1)}, bf16[2,128,512]{2,1,0:T(8,128)(2,1)S(1)}, u32[]{:S(2)}, u32[]{:S(2)}) collective-permute-start(bf16[2,128,512]{2,1,0:T(8,128)(2,1)S(1)} %get-tuple-element.13), channel_id=1, source_target_pairs={{0,4},{4,8},{8,12},{12,16},{16,20},{20,24},{24,28},{28,32},{32,36}... | collective-permute-start | bytes 786440 | tf_op jit(solution)/shard_map/ppermute | solution.py:20
  104.9 45.2 %collective-permute-start.3 = (bf16[2,128,512]{2,1,0:T(8,128)(2,1)S(1)}, bf16[2,128,512]{2,1,0:T(8,128)(2,1)S(1)}, u32[]{:S(2)}, u32[]{:S(2)}) collective-permute-start(bf16[2,128,512]{2,1,0:T(8,128)(2,1)S(1)} %get-tuple-element.14), channel_id=1, source_target_pairs={{4,0},{8,4},{12,8},{16,12},{20,16},{24,20},{28,24},{32,28},{36,32}... | collective-permute-start | bytes 786440 | tf_op jit(solution)/shard_map/ppermute | solution.py:21
  154.9 6.5 %copy-start.27 = (f32[128,512]{1,0:T(8,128)S(1)}, f32[128,512]{1,0:T(8,128)}, u32[]{:S(2)}) copy-start(f32[128,512]{1,0:T(8,128)} %convolution_add_fusion.11) | copy-start | bytes 786436
  154.9 6.5 %copy-start.29 = (f32[128,512]{1,0:T(8,128)S(1)}, f32[128,512]{1,0:T(8,128)}, u32[]{:S(2)}) copy-start(f32[128,512]{1,0:T(8,128)} %convolution_add_fusion.10) | copy-start | bytes 786436
  156.1 6.7 %copy-start.17 = (f32[1,128,1024]{2,1,0:T(8,128)S(1)}, f32[1,128,1024]{2,1,0:T(8,128)}, u32[]{:S(2)}) copy-start(f32[1,128,1024]{2,1,0:T(8,128)} %copy-done.16) | copy-start | bytes 1572868
  156.1 6.7 %copy-start.19 = (f32[1,128,1024]{2,1,0:T(8,128)S(1)}, f32[1,128,1024]{2,1,0:T(8,128)}, u32[]{:S(2)}) copy-start(f32[1,128,1024]{2,1,0:T(8,128)} %copy-done.18) | copy-start | bytes 1572868
  169.2 21.2 %all-to-all-start.2 = ((f32[64,2,128,8]{2,3,1,0:T(8,128)}), f32[64,2,128,8]{2,3,1,0:T(8,128)S(1)}, u32[]{:S(2)}, u32[]{:S(2)}) async-start(f32[64,2,128,8]{2,3,1,0:T(8,128)} %copy.53), calls=%async_computation.2 | async-start | bytes 1048576 | tf_op jit(solution)/shard_map/all_to_all | solution.py:49
  191.1 12.3 %all-to-all-start.3 = ((f32[4,1,8]{2,1,0:T(1,128)}), f32[4,1,8]{2,1,0:T(1,128)S(1)}, u32[]{:S(2)}, u32[]{:S(2)}) async-start(f32[4,1,8]{2,1,0:T(1,128)} %broadcast_in_dim.12), calls=%async_computation.3 | async-start | bytes 4096 | tf_op jit(solution)/shard_map/all_to_all | solution.py:34
  203.5 21.6 %all-to-all-start.6 = ((bf16[64,2,2304]{2,1,0:T(2,128)(2,1)}), bf16[64,2,2304]{2,1,0:T(2,128)(2,1)S(1)}, u32[]{:S(2)}, u32[]{:S(2)}) async-start(bf16[64,2,2304]{2,1,0:T(2,128)(2,1)} %reshape.197), calls=%async_computation.6 | async-start | bytes 1179648 | tf_op jit(solution)/shard_map/all_to_all | solution.py:99
  209.0 40.8 %copy-start.51 = (f32[8]{0:T(128)}, f32[8]{0:T(128)S(1)}, u32[]{:S(2)}) copy-start(f32[8]{0:T(128)S(1)} %get-tuple-element.4) | copy-start | bytes 100
  225.8 18.4 %all-to-all-start.4 = ((bf16[64,2,128,8]{2,3,1,0:T(8,128)(2,1)}), bf16[64,2,128,8]{2,3,1,0:T(8,128)(2,1)S(1)}, u32[]{:S(2)}, u32[]{:S(2)}) async-start(bf16[64,2,128,8]{2,3,1,0:T(8,128)(2,1)} %broadcast_in_dim.13), calls=%async_computation.4 | async-start | bytes 524288 | tf_op jit(solution)/shard_map/all_to_all | solution.py:34
  235.8 15.1 %slice-start.2 = ((s8[6291456]{0:T(1024)(128)(4,1)}), s8[2097152]{0:T(1024)(128)(4,1)S(1)}, s32[]{:S(2)}) async-start(s8[6291456]{0:T(1024)(128)(4,1)} %bitcast.647), calls=%async_computation.9 | async-start | bytes 4194304
  250.2 8.4 %copy-start.6 = (f32[1,128,1024]{2,1,0:T(8,128)}, f32[1,128,1024]{2,1,0:T(8,128)S(1)}, u32[]{:S(2)}) copy-start(f32[1,128,1024]{2,1,0:T(8,128)S(1)} %fusion.1) | copy-start | bytes 1572868
  258.7 18.0 %slice-start.4 = ((s8[6291456]{0:T(1024)(128)(4,1)}), s8[2097152]{0:T(1024)(128)(4,1)S(1)}, s32[]{:S(2)}) async-start(s8[6291456]{0:T(1024)(128)(4,1)} %bitcast.649), calls=%async_computation.11 | async-start | bytes 4194304
  260.0 17.0 %copy-start.35 = (f32[128,512]{1,0:T(8,128)S(1)}, f32[128,512]{1,0:T(8,128)}, u32[]{:S(2)}) copy-start(f32[128,512]{1,0:T(8,128)} %fusion.181) | copy-start | bytes 786436
  260.0 53.1 %all-to-all-start.5 = ((bf16[64,2,128,48]{2,3,1,0:T(8,128)(2,1)}), bf16[64,2,128,48]{2,3,1,0:T(8,128)(2,1)}, u32[]{:S(2)}, u32[]{:S(2)}) async-start(bf16[64,2,128,48]{2,3,1,0:T(8,128)(2,1)} %broadcast_in_dim.14), calls=%async_computation.5 | async-start | bytes 3145728 | tf_op jit(solution)/shard_map/all_to_all | solution.py:34
  268.2 7.1 %copy-start.37 = (f32[128,512]{1,0:T(8,128)S(1)}, f32[128,512]{1,0:T(8,128)}, u32[]{:S(2)}) copy-start(f32[128,512]{1,0:T(8,128)} %fusion.191) | copy-start | bytes 786436
  268.2 8.5 %copy-start.36 = (f32[128,512]{1,0:T(8,128)S(1)}, f32[128,512]{1,0:T(8,128)}, u32[]{:S(2)}) copy-start(f32[128,512]{1,0:T(8,128)} %fusion.137) | copy-start | bytes 786436
  269.7 7.0 %slice-start.5 = ((s8[6291456]{0:T(1024)(128)(4,1)}), s8[4194304]{0:T(1024)(128)(4,1)S(1)}, s32[]{:S(2)}) async-start(s8[6291456]{0:T(1024)(128)(4,1)} %bitcast.649), calls=%async_computation.12 | async-start | bytes 8388608
  274.2 9.6 %copy-start.8 = (f32[1,128,1024]{2,1,0:T(8,128)}, f32[1,128,1024]{2,1,0:T(8,128)S(1)}, u32[]{:S(2)}) copy-start(f32[1,128,1024]{2,1,0:T(8,128)S(1)} %maximum_bitcast_fusion.7) | copy-start | bytes 1572868
  274.2 9.9 %copy-start.10 = (f32[1,128,1024]{2,1,0:T(8,128)}, f32[1,128,1024]{2,1,0:T(8,128)S(1)}, u32[]{:S(2)}) copy-start(f32[1,128,1024]{2,1,0:T(8,128)S(1)} %maximum_bitcast_fusion.8) | copy-start | bytes 1572868
  274.3 37.9 %collective-permute-start.4 = (bf16[2,128,512]{2,1,0:T(8,128)(2,1)S(1)}, bf16[2,128,512]{2,1,0:T(8,128)(2,1)S(1)}, u32[]{:S(2)}, u32[]{:S(2)}) collective-permute-start(bf16[2,128,512]{2,1,0:T(8,128)(2,1)S(1)} %fusion.90), channel_id=1, source_target_pairs={{0,4},{4,8},{8,12},{12,16},{16,20},{20,24},{24,28},{28,32},{32,36}... | collective-permute-start | bytes 786440 | tf_op jit(solution)/shard_map/ppermute | solution.py:20
  277.4 8.3 %copy-start.12 = (f32[1,128,1024]{2,1,0:T(8,128)}, f32[1,128,1024]{2,1,0:T(8,128)S(1)}, u32[]{:S(2)}) copy-start(f32[1,128,1024]{2,1,0:T(8,128)S(1)} %maximum_bitcast_fusion.9) | copy-start | bytes 1572868
  278.1 7.7 %copy-start.14 = (f32[1,128,1024]{2,1,0:T(8,128)}, f32[1,128,1024]{2,1,0:T(8,128)S(1)}, u32[]{:S(2)}) copy-start(f32[1,128,1024]{2,1,0:T(8,128)S(1)} %maximum_bitcast_fusion.10) | copy-start | bytes 1572868
  278.1 34.1 %collective-permute-start.5 = (bf16[2,128,512]{2,1,0:T(8,128)(2,1)S(1)}, bf16[2,128,512]{2,1,0:T(8,128)(2,1)S(1)}, u32[]{:S(2)}, u32[]{:S(2)}) collective-permute-start(bf16[2,128,512]{2,1,0:T(8,128)(2,1)S(1)} %fusion.88), channel_id=1, source_target_pairs={{4,0},{8,4},{12,8},{16,12},{20,16},{24,20},{28,24},{32,28},{36,32}... | collective-permute-start | bytes 786440 | tf_op jit(solution)/shard_map/ppermute | solution.py:21
  315.2 7.5 %copy-start.7 = (f32[1,128,1024]{2,1,0:T(8,128)S(1)}, f32[1,128,1024]{2,1,0:T(8,128)}, u32[]{:S(2)}) copy-start(f32[1,128,1024]{2,1,0:T(8,128)} %copy-done.6) | copy-start | bytes 1572868
  315.2 7.5 %copy-start.9 = (f32[1,128,1024]{2,1,0:T(8,128)S(1)}, f32[1,128,1024]{2,1,0:T(8,128)}, u32[]{:S(2)}) copy-start(f32[1,128,1024]{2,1,0:T(8,128)} %copy-done.8) | copy-start | bytes 1572868
  315.2 7.5 %copy-start.11 = (f32[1,128,1024]{2,1,0:T(8,128)S(1)}, f32[1,128,1024]{2,1,0:T(8,128)}, u32[]{:S(2)}) copy-start(f32[1,128,1024]{2,1,0:T(8,128)} %copy-done.10) | copy-start | bytes 1572868
  315.2 7.5 %copy-start.13 = (f32[1,128,1024]{2,1,0:T(8,128)S(1)}, f32[1,128,1024]{2,1,0:T(8,128)}, u32[]{:S(2)}) copy-start(f32[1,128,1024]{2,1,0:T(8,128)} %copy-done.12) | copy-start | bytes 1572868
  315.2 7.5 %copy-start.15 = (f32[1,128,1024]{2,1,0:T(8,128)S(1)}, f32[1,128,1024]{2,1,0:T(8,128)}, u32[]{:S(2)}) copy-start(f32[1,128,1024]{2,1,0:T(8,128)} %copy-done.14) | copy-start | bytes 1572868
  315.2 7.5 %copy-start.20 = (f32[2,128,512]{2,1,0:T(8,128)S(1)}, f32[2,128,512]{2,1,0:T(8,128)}, u32[]{:S(2)}) copy-start(f32[2,128,512]{2,1,0:T(8,128)} %get-tuple-element.12) | copy-start | bytes 1572868
  (24 other events, 106.5 us)
where the time goes:
time: 330 us; the launch traced here: 325 us
  matrix products  123 us (37%)
  waiting for transfers between devices  90.7 us (27%)
  starting transfers between devices  72 us (22%)
  local copies, waits for them, and re-layouts  28.2 us (9%)
  other arithmetic  7.61 us (2%)
    dot_general x142, matrix products, plain_dot(): lax.dot_general(left, right, (((1,), (contract,)), ((), ())), preferred_e...  121 us
    ppermute x3, waiting for transfers between devices, extended(): before = lax.ppermute(last, axis, up)  56.7 us
    all_to_all x5, starting transfers between devices, from_everyone(): lax.all_to_all(jnp.broadcast_to(x[None], (length, *x.shape)), axis, 0, 0,...  43 us
    all_to_all x1, waiting for transfers between devices, per_device(): lax.all_to_all(masked, 'tile', split_axis=1, concat_axis=2, tiled=True)  15.9 us
    ppermute x3, starting transfers between devices, extended(): after = lax.ppermute(initial, axis, down)  15.1 us
    all_to_all x1, waiting for transfers between devices, sum_at_owner(): blocks = lax.all_to_all(split_up(x, dim, length), axis, 0, 0, tiled=True)  13.5 us
  transfers between devices with their start and end apart: 13, of which 7 were waited for; matrix products, arithmetic and copies ran while one was open for 27% of the time, Pallas kernels for 0%

commit v1 on v0

v1 whole, which is shorter than its diff:
```python
import functools

import jax
import jax.numpy as jnp
from jax import lax
from jax.experimental import pallas as pl
from jax.experimental.pallas import tpu as pltpu
from jax.sharding import PartitionSpec as P

TILE = 512
RANK = 24
PAIR = 2 * RANK
ROWS = 128
DAMPING = 0.8
HALF = 256
F32 = jnp.float32
BF16 = jnp.bfloat16


def dot(left, right):
    return lax.dot_general(left, right, (((1,), (0,)), ((), ())), preferred_element_type=F32)


def dot_nt(left, right):
    return lax.dot_general(left, right, (((1,), (1,)), ((), ())), preferred_element_type=F32)


def rows_joined(by_re, by_im):
    return jnp.concatenate(
        [by_re[:ROWS] - by_im[ROWS:], by_re[ROWS:] + by_im[:ROWS]], axis=0
    )


def lanes_joined(by_re, by_im):
    return jnp.concatenate(
        [by_re[:, :ROWS] - by_im[:, ROWS:], by_re[:, ROWS:] + by_im[:, :ROWS]], axis=1
    )


def aligned(start, size, unit):
    return pl.ds(pl.multiple_of(start, unit), size)


def kernel(
    nz,
    nq,
    ns,
    exc,
    near_hbm,
    sbasis,
    tbasis,
    coup,
    rank,
    link,
    fk_hbm,
    target,
    owner,
    field_out,
    res_out,
    adj_out,
    near,
    fk,
    vb,
    halo,
    nacc,
    mt_send,
    mt,
    mback,
    gath,
    part,
    parts_in,
    fsend,
    fparts,
    fz,
    fzparts,
    isum,
    iparts,
    wz,
    wg,
    wt,
    rrow,
    rgath,
    edge_send,
    edge_in,
    local_sem,
    s_halo,
    r_halo,
    s_mt,
    r_mt,
    s_gath,
    r_gath,
    s_part,
    r_part,
    s_f,
    r_f,
    s_fz,
    r_fz,
    s_i,
    r_i,
    s_w,
    r_w,
    s_wg,
    r_wg,
    s_rr,
    r_rr,
    s_edge,
    r_edge,
):
    t = lax.axis_index("tile")
    s = lax.axis_index("src")
    nt = nz * nq
    q = t // nz
    z = t - q * nz
    tiles = 2 * nt
    group = nz * PAIR
    spread = nq * PAIR
    fgroup = nz * 8
    focal_count = nt * 8

    def z_peer(d):
        return q * nz + lax.rem(z + d, nz)

    def q_peer(d):
        return lax.rem(q + d, nq) * nz + z

    left = lax.rem(t + nt - 1, nt)
    right = lax.rem(t + 1, nt)

    barrier = pltpu.get_barrier_semaphore()
    count = 0
    for d in range(1, nz):
        pl.semaphore_signal(barrier, inc=1, device_id={"tile": z_peer(d), "src": s})
        count += 1
    for d in range(1, nq):
        pl.semaphore_signal(barrier, inc=1, device_id={"tile": q_peer(d), "src": s})
        count += 1
    for other in (left, right):
        pl.semaphore_signal(barrier, inc=1, device_id={"tile": other, "src": s})
        count += 1
    for d in range(1, ns):
        pl.semaphore_signal(barrier, inc=1, device_id={"tile": t, "src": lax.rem(s + d, ns)})
        count += 1

    near_copy = pltpu.make_async_copy(near_hbm, near, local_sem.at[0])
    near_copy.start()
    fk_copy = pltpu.make_async_copy(fk_hbm, fk, local_sem.at[1])
    fk_copy.start()

    pending = []

    def send(src_ref, dst_ref, send_sem, recv_sem, tile=None, src=None):
        copy = pltpu.make_async_remote_copy(
            src_ref=src_ref,
            dst_ref=dst_ref,
            send_sem=send_sem,
            recv_sem=recv_sem,
            device_id={"tile": t if tile is None else tile, "src": s if src is None else src},
        )
        copy.start()
        pending.append(copy)

    def arrived(ref, send_sem, recv_sem):
        pltpu.make_async_remote_copy(
            src_ref=ref,
            dst_ref=ref,
            send_sem=send_sem,
            recv_sem=recv_sem,
            device_id={"tile": right, "src": s},
        ).wait_recv()

    def far_order(n):
        return sorted(range(1, n), key=lambda d: -min(d, n - d))

    def own_slice(index):
        return aligned(index * PAIR, PAIR, 16)

    def projected(x, basis):
        pieces = []
        for l in range(2):
            both = dot_nt(basis[l], x[:, l * TILE : (l + 1) * TILE])
            pieces.append(lanes_joined(both[:RANK], both[RANK:]))
        return jnp.concatenate(pieces, axis=0).astype(BF16)

    def gather(stage, value, along_z):
        n, mine = (nz, z) if along_z else (nq, q)
        here = gath.at[stage, own_slice(mine)]
        gath[stage, own_slice(mine), :] = value
        for d in far_order(n):
            send(
                here,
                here,
                s_gath.at[stage, d],
                r_gath.at[stage, d],
                tile=z_peer(d) if along_z else q_peer(d),
            )

    def gathered(stage, along_z):
        n, mine = (nz, z) if along_z else (nq, q)
        for d in range(1, n):
            sender = lax.rem(mine + n - d, n)
            arrived(
                gath.at[stage, own_slice(sender)], s_gath.at[stage, d], r_gath.at[stage, d]
            )

    def scatter(stage, value, along_z):
        n, mine = (nz, z) if along_z else (nq, q)
        part[stage] = value.astype(BF16)
        for d in far_order(n):
            owner_of = lax.rem(mine + d, n)
            send(
                part.at[stage, own_slice(owner_of)],
                parts_in.at[stage, d],
                s_part.at[stage, d],
                r_part.at[stage, d],
                tile=z_peer(d) if along_z else q_peer(d),
            )

    def scattered(stage, along_z):
        n, mine = (nz, z) if along_z else (nq, q)
        total = part[stage, own_slice(mine), :].astype(F32)
        for d in range(1, n):
            arrived(parts_in.at[stage, d], s_part.at[stage, d], r_part.at[stage, d])
            total = total + parts_in[stage, d].astype(F32)
        return total.astype(BF16).astype(F32)

    def expanded(coefficients, basis, l):
        piece = coefficients[l * RANK : (l + 1) * RANK]
        turned = jnp.concatenate([-piece[:, ROWS:], piece[:, :ROWS]], axis=1)
        stacked = jnp.concatenate([piece, turned], axis=0)
        return dot(jnp.transpose(stacked).astype(BF16), basis[l])

    def send_halo(stage):
        send(
            vb.at[stage, :, TILE : 2 * TILE],
            halo.at[stage, 0],
            s_halo.at[stage, 0],
            r_halo.at[stage, 0],
            tile=right,
        )
        send(
            vb.at[stage, :, 0:TILE],
            halo.at[stage, 1],
            s_halo.at[stage, 1],
            r_halo.at[stage, 1],
            tile=left,
        )

    vb[0] = exc[...]
    first_coeff = projected(exc[...], sbasis)

    level = lax.broadcasted_iota(jnp.int32, (RANK, tiles), 0)
    source_tile = lax.broadcasted_iota(jnp.int32, (1, tiles), 1)
    limits = []
    for l in range(2):
        gap = t * 2 + l - source_tile
        is_near = (
            (gap == 0)
            | (gap == 1)
            | (gap == -1)
            | (gap == tiles - 1)
            | (gap == 1 - tiles)
        )
        here = jnp.where((link[l : l + 1, :] == 1) & ~is_near, rank[l : l + 1, :], 0)
        wide = jnp.broadcast_to(here, (RANK, tiles))
        limits.append(jnp.where(level < wide, wide, 0).astype(F32))
    limits.append(
        jnp.broadcast_to(source_tile, (16, tiles)).astype(F32)
    )
    limit_rows = jnp.concatenate(limits, axis=0).astype(BF16)

    pl.semaphore_wait(barrier, count)

    gather(0, first_coeff, True)
    send_halo(0)

    tile_row = lax.broadcasted_iota(jnp.int32, (tiles, group), 0)
    lane = lax.broadcasted_iota(jnp.int32, (tiles, group), 1)
    lane_row = lax.broadcasted_iota(jnp.int32, (1, group), 1)
    for d in far_order(nq) + [0]:
        to = lax.rem(q + d, nq)
        offset = lane - (tile_row - to * (2 * nz)) * RANK
        pick = jnp.where((offset >= 0) & (offset < RANK), 1.0, 0.0).astype(BF16)
        limit = dot(limit_rows, pick)
        position = (lane_row + to * group).astype(F32) - limit[PAIR : PAIR + 1, :] * float(RANK)
        keep = position < limit[:PAIR]
        for c in range(2):
            block = coup[c, :, aligned(to * group, group, 128)]
            block = jnp.where(keep, block.astype(F32), 0.0).astype(BF16)
            if d == 0:
                mt[c, own_slice(q), :] = block
            else:
                mt_send[d, c] = block
        if d != 0:
            send(
                mt_send.at[d],
                mt.at[:, own_slice(q), :],
                s_mt.at[d],
                r_mt.at[d],
                tile=q_peer(d),
            )

    def near_own(stage):
        @pl.loop(0, 4)
        def _(step):
            i = step // 2
            cols = aligned((step % 2) * HALF, HALF, HALF)
            by_re = jnp.zeros((2 * ROWS, HALF), F32)
            by_im = jnp.zeros((2 * ROWS, HALF), F32)
            for l in range(2):
                x = vb[stage, :, l * TILE : (l + 1) * TILE]
                by_re = by_re + dot(x, near[i, l - i + 1, 0, :, cols])
                by_im = by_im + dot(x, near[i, l - i + 1, 1, :, cols])
            nacc[:, aligned(step * HALF, HALF, HALF)] = rows_joined(by_re, by_im)

    def near_halo(stage):
        @pl.loop(0, 4)
        def _(step):
            i = step // 2
            cols = aligned((step % 2) * HALF, HALF, HALF)
            x = halo[stage, i]
            by_re = dot(x, near[i, 2 * i, 0, :, cols])
            by_im = dot(x, near[i, 2 * i, 1, :, cols])
            out = aligned(step * HALF, HALF, HALF)
            nacc[:, out] = nacc[:, out] + rows_joined(by_re, by_im)

    near_copy.wait()
    for stage in range(2):
        if stage == 1:
            gather(1, projected(vb[1], sbasis), True)
            send_halo(1)
        near_own(stage)
        gathered(stage, True)
        if stage == 0:
            for d in range(1, nq):
                sender = lax.rem(q + nq - d, nq)
                arrived(mt.at[:, own_slice(sender), :], s_mt.at[d], r_mt.at[d])
        coefficients = gath[stage, :group, :]
        scatter(
            stage,
            lanes_joined(dot(mt[0], coefficients), dot(mt[1], coefficients)),
            False,
        )
        for side in range(2):
            arrived(halo.at[stage, side], s_halo.at[stage, side], r_halo.at[stage, side])
        near_halo(stage)
        if stage == 0:
            for c in range(2):
                mback[c] = jnp.transpose(mt[c].astype(F32)).astype(BF16)
        coupled = scattered(stage, False)
        for l in range(2):
            cols = slice(l * TILE, (l + 1) * TILE)
            added = nacc[:, cols] + expanded(coupled, tbasis, l)
            right_side = exc[:, cols].astype(F32)
            if stage == 0:
                value = right_side - DAMPING * added
            else:
                before = field_out[:, cols]
                value = before + DAMPING * (right_side - (before + added))
            field_out[:, cols] = value
            vb[stage + 1, :, cols] = value.astype(BF16)

    fk_copy.wait()
    x = vb[2]
    fsend[...] = lanes_joined(dot_nt(fk[0], x), dot_nt(fk[1], x))

    def f_rows(index):
        return aligned(index * fgroup, fgroup, 8)

    for d in far_order(nq):
        send(
            fsend.at[f_rows(lax.rem(q + d, nq))],
            fparts.at[d],
            s_f.at[d],
            r_f.at[d],
            tile=q_peer(d),
        )
    total = fsend[f_rows(q), :]
    for d in range(1, nq):
        arrived(fparts.at[d], s_f.at[d], r_f.at[d])
        total = total + fparts[d]
    fz[...] = total

    def z_rows(index):
        return aligned(index * 8, 8, 8)

    for d in far_order(nz):
        send(
            fz.at[z_rows(lax.rem(z + d, nz))],
            fzparts.at[d],
            s_fz.at[d],
            r_fz.at[d],
            tile=z_peer(d),
        )
    focal = fz[z_rows(z), :]
    for d in range(1, nz):
        arrived(fzparts.at[d], s_fz.at[d], r_fz.at[d])
        focal = focal + fzparts[d]
    square = focal * focal
    strength = jnp.sum(square[:, :ROWS] + square[:, ROWS:], axis=1, keepdims=True)
    isum[...] = jnp.broadcast_to(strength, (8, 128))
    for d in range(1, ns):
        send(isum, iparts.at[d], s_i.at[d], r_i.at[d], src=lax.rem(s + d, ns))
    slot = lax.broadcasted_iota(jnp.int32, (8, focal_count), 0)
    spot = lax.broadcasted_iota(jnp.int32, (8, focal_count), 1)
    wanted = jnp.sum(
        jnp.where(spot == slot + t * 8, jnp.broadcast_to(target[...], (8, focal_count)), 0.0),
        axis=1,
        keepdims=True,
    )
    strength = isum[...]
    for d in range(1, ns):
        arrived(iparts.at[d], s_i.at[d], r_i.at[d])
        strength = strength + iparts[d]
    residual = jnp.tanh(strength / (2.0 * ROWS * ns)) - wanted
    wz[z_rows(z), :] = jnp.concatenate(
        [residual * focal[:, :ROWS], -residual * focal[:, ROWS:], residual], axis=1
    )
    for d in far_order(nz):
        here = wz.at[z_rows(z)]
        send(here, here, s_w.at[d], r_w.at[d], tile=z_peer(d))
    for d in range(1, nz):
        sender = lax.rem(z + nz - d, nz)
        arrived(wz.at[z_rows(sender)], s_w.at[d], r_w.at[d])
    f16 = aligned(q * fgroup, fgroup, 16)
    wg[f16, :] = wz[:, : 2 * ROWS].astype(BF16)
    for d in far_order(nq):
        here = wg.at[f16]
        send(here, here, s_wg.at[d], r_wg.at[d], tile=q_peer(d))
    row = lax.broadcasted_iota(jnp.int32, (fgroup, 128), 0)
    lane128 = lax.broadcasted_iota(jnp.int32, (fgroup, 128), 1)
    shift = lax.rem(q * fgroup, 128)
    flat = jnp.sum(
        jnp.where(lane128 == row + shift, wz[:, 2 * ROWS :], 0.0), axis=0, keepdims=True
    )
    rrow[...] = jnp.broadcast_to(flat, (8, 128))
    rgath[q] = jnp.broadcast_to(flat, (8, 128))
    for d in far_order(nq):
        send(rrow, rgath.at[q], s_rr.at[d], r_rr.at[d], tile=q_peer(d))
    for d in range(1, nq):
        sender = lax.rem(q + nq - d, nq)
        arrived(wg.at[aligned(sender * fgroup, fgroup, 16)], s_wg.at[d], r_wg.at[d])
    wt[...] = jnp.transpose(wg[...].astype(F32)).astype(BF16)

    scale = float(tiles * TILE / focal_count) ** 0.5

    @pl.loop(0, 4)
    def _(step):
        cols = aligned(step * HALF, HALF, HALF)
        w = wt[...]
        u = rows_joined(dot(w, fk[0, :, cols]), dot(w, fk[1, :, cols])) * scale
        adj_out[:, cols] = u
        vb[3, :, cols] = u.astype(BF16)

    gather(2, projected(vb[3], tbasis), False)

    @pl.loop(0, 4)
    def _(step):
        i = step // 2
        half = aligned((step % 2) * HALF, HALF, HALF)
        x = vb[3, :, aligned(i * TILE, TILE, TILE)]
        by_re = dot_nt(x, near[i, 2 * i, 0, half, :])
        by_im = dot_nt(x, near[i, 2 * i, 1, half, :])
        edge_send[i, :, half] = rows_joined(by_re, by_im).astype(BF16)

    send(edge_send.at[0], edge_in.at[1], s_edge.at[0], r_edge.at[1], tile=left)
    send(edge_send.at[1], edge_in.at[0], s_edge.at[1], r_edge.at[0], tile=right)

    gathered(2, False)
    coefficients = gath[2, :spread, :]
    scatter(
        2,
        lanes_joined(dot(mback[0], coefficients), dot(mback[1], coefficients)),
        True,
    )

    @pl.loop(0, 4)
    def _(step):
        m = step // 2
        half = aligned((step % 2) * HALF, HALF, HALF)
        by_re = jnp.zeros((2 * ROWS, HALF), F32)
        by_im = jnp.zeros((2 * ROWS, HALF), F32)
        for i in range(2):
            x = vb[3, :, i * TILE : (i + 1) * TILE]
            by_re = by_re + dot_nt(x, near[i, m - i + 1, 0, half, :])
            by_im = by_im + dot_nt(x, near[i, m - i + 1, 1, half, :])
        nacc[:, aligned(step * HALF, HALF, HALF)] = rows_joined(by_re, by_im)

    back = scattered(2, True)
    for side in range(2):
        arrived(edge_in.at[side], s_edge.at[side], r_edge.at[side])
    for l in range(2):
        cols = slice(l * TILE, (l + 1) * TILE)
        added = nacc[:, cols] + edge_in[l].astype(F32) + expanded(back, sbasis, l)
        adj_out[:, cols] = adj_out[:, cols] - DAMPING * added

    lines = (focal_count + 127) // 128
    for d in range(1, nq):
        sender = lax.rem(q + nq - d, nq)
        arrived(rgath.at[sender], s_rr.at[d], r_rr.at[d])
    mine = lax.broadcasted_iota(jnp.int32, (8, 128), 0) + t * 8
    found = jnp.zeros((8, 128), F32)
    for line in range(lines):
        values = jnp.zeros((8, 128), F32)
        for other in range(nq):
            if other * fgroup // 128 == line:
                values = values + rgath[other]
        owners = jnp.broadcast_to(owner[line : line + 1, :], (8, 128))
        found = found + jnp.where(owners == mine, values, 0.0)
    res_out[...] = jnp.broadcast_to(jnp.sum(found, axis=1, keepdims=True), (8, 128))

    for copy in pending:
        copy.wait_send()


def per_device(
    nz,
    excitation,
    near_blocks,
    source_basis,
    target_basis,
    coupling,
    pair_rank,
    far_link,
    focal_kernel,
    focal_target,
    focal_owner,
):
    nt = lax.axis_size("tile")
    ns = lax.axis_size("src")
    nq = nt // nz
    focal_count = focal_target.shape[0]
    group = nz * PAIR
    spread = nq * PAIR
    fgroup = nz * 8
    width = 2 * TILE
    most = max(nz, nq)
    lines = (focal_count + 127) // 128
    owner = jnp.pad(focal_owner, (0, lines * 128 - focal_count), constant_values=-1)
    vmem = pl.BlockSpec(memory_space=pltpu.VMEM)
    anywhere = pl.BlockSpec(memory_space=pl.ANY)
    dma = pltpu.SemaphoreType.DMA
    both = 2 * ROWS
    field, residual, adjoint = pl.pallas_call(
        functools.partial(kernel, nz, nq, ns),
        out_shape=(
            jax.ShapeDtypeStruct((both, width), F32),
            jax.ShapeDtypeStruct((8, 128), F32),
            jax.ShapeDtypeStruct((both, width), F32),
        ),
        in_specs=[vmem, anywhere, vmem, vmem, vmem, vmem, vmem, anywhere, vmem, vmem],
        out_specs=(vmem, vmem, vmem),
        scratch_shapes=[
            pltpu.VMEM((2, 3, 2, TILE, TILE), BF16),
            pltpu.VMEM((2, focal_count, width), BF16),
            pltpu.VMEM((4, both, width), BF16),
            pltpu.VMEM((2, 2, both, TILE), BF16),
            pltpu.VMEM((both, width), F32),
            pltpu.VMEM((nq, 2, PAIR, group), BF16),
            pltpu.VMEM((2, spread, group), BF16),
            pltpu.VMEM((2, group, spread), BF16),
            pltpu.VMEM((3, most * PAIR, both), BF16),
            pltpu.VMEM((3, most * PAIR, both), BF16),
            pltpu.VMEM((3, most, PAIR, both), BF16),
            pltpu.VMEM((focal_count, both), F32),
            pltpu.VMEM((nq, fgroup, both), F32),
            pltpu.VMEM((fgroup, both), F32),
            pltpu.VMEM((nz, 8, both), F32),
            pltpu.VMEM((8, 128), F32),
            pltpu.VMEM((ns, 8, 128), F32),
            pltpu.VMEM((fgroup, 3 * ROWS), F32),
            pltpu.VMEM((focal_count, both), BF16),
            pltpu.VMEM((both, focal_count), BF16),
            pltpu.VMEM((8, 128), F32),
            pltpu.VMEM((nq, 8, 128), F32),
            pltpu.VMEM((2, both, TILE), BF16),
            pltpu.VMEM((2, both, TILE), BF16),
            dma((2,)),
            dma((2, 2)),
            dma((2, 2)),
            dma((nq,)),
            dma((nq,)),
            dma((3, most)),
            dma((3, most)),
            dma((3, most)),
            dma((3, most)),
            dma((nq,)),
            dma((nq,)),
            dma((nz,)),
            dma((nz,)),
            dma((ns,)),
            dma((ns,)),
            dma((nz,)),
            dma((nz,)),
            dma((nq,)),
            dma((nq,)),
            dma((nq,)),
            dma((nq,)),
            dma((2,)),
            dma((2,)),
        ],
        compiler_params=pltpu.CompilerParams(
            collective_id=0, has_side_effects=True, vmem_limit_bytes=48 * 1024 * 1024
        ),
    )(
        excitation.reshape(both, width),
        near_blocks,
        source_basis.reshape(2, PAIR, TILE),
        target_basis.reshape(2, PAIR, TILE),
        jnp.swapaxes(coupling, 1, 2),
        pair_rank.T,
        far_link.T,
        focal_kernel,
        focal_target.reshape(1, focal_count),
        owner.reshape(lines, 128),
    )
    return (
        field.reshape(2, ROWS, width),
        residual[:, 0],
        adjoint.reshape(2, ROWS, width),
    )


def solution(mesh):
    nt = mesh.shape["tile"]
    nz = 8 if nt % 8 == 0 and nt > 8 else 2
    return jax.shard_map(
        functools.partial(per_device, nz),
        mesh=mesh,
        in_specs=(
            P(None, "src", "tile"),
            P("tile", None, None, None, None),
            P("tile", None, None, None),
            P("tile", None, None, None),
            P(None, None, "tile"),
            P(None, "tile"),
            P(None, "tile"),
            P(None, None, "tile"),
            P(),
            P(),
        ),
        out_specs=(P(None, "src", "tile"), P("tile"), P(None, "src", "tile")),
        check_vma=False,
    )
```

time: 330 us -> 96.9 us (0.29)
  the two profiles are of different devices: /device:TPU:1 before, /device:TPU:2 now
where the time goes in v1:
time: 96.9 us; the launch traced here: 96.6 us
  Pallas kernels  85.2 us (88%)
  local copies, waits for them, and re-layouts  10.8 us (11%)
    pallas_call x1, Pallas kernels, per_device(): pl.pallas_call(functools.partial(kernel, nz, nq, ns), out_shape=(jax.Shap...  85.2 us
    unnamed x20, local copies, waits for them, and re-layouts  10.1 us

profile of v1, /device:TPU:2, one launch (start us, length us, event | category | flops | bytes accessed | tf_op | source)
XLA Modules:
  0.0 96.6 jit_solution(4107019418279782034)
XLA Ops:
  0.6 0.0 copy-start
  0.6 1.6 %copy-done = bf16[2,512,1024]{2,1,0:T(8,128)(2,1)S(1)} copy-done((bf16[2,512,1024]{2,1,0:T(8,128)(2,1)S(1)}, bf16[2,512,1024]{2,1,0:T(8,128)(2,1)}, u32[]{:S(2)}) %copy-start) | copy-done | bytes 2097176
  2.2 0.0 copy-start.1
  2.2 1.1 %copy-done.1 = bf16[2,3072,48]{1,2,0:T(8,128)(2,1)S(1)} copy-done((bf16[2,3072,48]{1,2,0:T(8,128)(2,1)S(1)}, bf16[2,3072,48]{1,2,0:T(8,128)(2,1)}, u32[]{:S(2)}) %copy-start.1) | copy-done | bytes 589848
  3.3 0.0 copy-start.2
  3.3 1.0 %copy-done.2 = bf16[2,128,1024]{2,1,0:T(8,128)(2,1)S(1)} copy-done((bf16[2,128,1024]{2,1,0:T(8,128)(2,1)S(1)}, bf16[2,128,1024]{2,1,0:T(8,128)(2,1)}, u32[]{:S(2)}) %copy-start.2) | copy-done | bytes 524312
  4.3 0.0 copy-start.3
  4.3 0.9 copy-done.3
  5.2 0.0 copy-start.4
  5.2 0.9 copy-done.4
  6.1 0.0 copy-start.5
  6.1 0.7 copy-done.5
  6.8 0.0 copy-start.6
  6.8 0.7 copy-done.6
  7.5 0.0 copy-start.7
  7.5 0.7 copy-done.7
  8.2 0.0 copy-start.8
  8.2 0.7 copy-done.8
  8.8 85.2 %shard_map.121 = (f32[256,1024]{1,0:T(8,128)S(1)}, f32[8,128]{1,0:T(8,128)S(1)}, f32[256,1024]{1,0:T(8,128)S(1)}) custom-call(bf16[256,1024]{1,0:T(8,128)(2,1)S(1)} %bitcast.13, bf16[2,3,2,512,512]{4,3,2,1,0:T(8,128)(2,1)} %near_hbm.1, bf16[2,48,512]{2,1,0:T(8,128)(2,1)S(1)} %bitcast.14, bf16[2,48,512]{2,1,0:T(8,128)(2,1)S(1)} %bitcast.15, ...), custom_call_target="tpu_custom_call" | custom-call | tf_op jit(solution)/shard_map/pallas_call | solution.py:543
  94.0 0.6 slice_reduce_fusion
  94.6 1.0 %copy.15 = f32[2,128,1024]{2,1,0:T(8,128)} copy(f32[2,128,1024]{2,1,0:T(8,128)S(1)} %bitcast.11) | data formatting | bytes 2097152
  95.6 1.0 %copy.16 = f32[2,128,1024]{2,1,0:T(8,128)} copy(f32[2,128,1024]{2,1,0:T(8,128)S(1)} %bitcast.10) | data formatting | bytes 2097152
Async XLA Ops:
  0.6 1.6 %copy-start = (bf16[2,512,1024]{2,1,0:T(8,128)(2,1)S(1)}, bf16[2,512,1024]{2,1,0:T(8,128)(2,1)}, u32[]{:S(2)}) copy-start(bf16[2,512,1024]{2,1,0:T(8,128)(2,1)} %fk_hbm.1) | copy-start | bytes 6291460
  2.2 1.1 %copy-start.1 = (bf16[2,3072,48]{1,2,0:T(8,128)(2,1)S(1)}, bf16[2,3072,48]{1,2,0:T(8,128)(2,1)}, u32[]{:S(2)}) copy-start(bf16[2,3072,48]{1,2,0:T(8,128)(2,1)} %param.14) | copy-start | bytes 1769476
  3.3 1.0 %copy-start.2 = (bf16[2,128,1024]{2,1,0:T(8,128)(2,1)S(1)}, bf16[2,128,1024]{2,1,0:T(8,128)(2,1)}, u32[]{:S(2)}) copy-start(bf16[2,128,1024]{2,1,0:T(8,128)(2,1)} %param.10) | copy-start | bytes 1572868
  4.3 0.9 copy-start.3
  5.2 0.9 copy-start.4
  6.1 0.7 copy-start.5
  6.8 0.7 copy-start.6
  7.5 0.7 copy-start.7
  8.2 0.7 copy-start.8

commit v2 on v1

--- a/solution.py
+++ b/solution.py
@@ -45,21 +45,30 @@
     nz,
     nq,
     ns,
-    exc,
+    exc_hbm,
     near_hbm,
+    sbasis_hbm,
+    tbasis_hbm,
+    coup_hbm,
+    rank_hbm,
+    link_hbm,
+    fk_hbm,
+    target_hbm,
+    owner_hbm,
+    field_out,
+    res_out,
+    adj_out,
+    field,
+    adjoint,
+    near,
+    fk,
     sbasis,
     tbasis,
     coup,
     rank,
     link,
-    fk_hbm,
     target,
     owner,
-    field_out,
-    res_out,
-    adj_out,
-    near,
-    fk,
     vb,
     halo,
     nacc,
@@ -75,7 +84,7 @@
     fzparts,
     isum,
     iparts,
-    wz,
+    fall,
     wg,
     wt,
     rrow,
@@ -99,6 +108,8 @@
     r_i,
     s_w,
     r_w,
+    s_sib,
+    r_sib,
     s_wg,
     r_wg,
     s_rr,
@@ -128,23 +139,41 @@
 
     barrier = pltpu.get_barrier_semaphore()
     count = 0
-    for d in range(1, nz):
-        pl.semaphore_signal(barrier, inc=1, device_id={"tile": z_peer(d), "src": s})
-        count += 1
     for d in range(1, nq):
         pl.semaphore_signal(barrier, inc=1, device_id={"tile": q_peer(d), "src": s})
         count += 1
     for other in (left, right):
         pl.semaphore_signal(barrier, inc=1, device_id={"tile": other, "src": s})
         count += 1
-    for d in range(1, ns):
-        pl.semaphore_signal(barrier, inc=1, device_id={"tile": t, "src": lax.rem(s + d, ns)})
-        count += 1
-
-    near_copy = pltpu.make_async_copy(near_hbm, near, local_sem.at[0])
-    near_copy.start()
-    fk_copy = pltpu.make_async_copy(fk_hbm, fk, local_sem.at[1])
-    fk_copy.start()
+    for e in range(ns):
+        for d in range(nz):
+            if d or e:
+                pl.semaphore_signal(
+                    barrier,
+                    inc=1,
+                    device_id={"tile": z_peer(d), "src": lax.rem(s + e, ns)},
+                )
+                count += 1
+    core = lax.rem(s, 2)
+    sibling = s + 1 - 2 * core
+
+    loads = {}
+    for k, (name, source, place) in enumerate(
+        (
+            ("exc", exc_hbm, vb.at[0]),
+            ("sbasis", sbasis_hbm, sbasis),
+            ("rank", rank_hbm, rank),
+            ("link", link_hbm, link),
+            ("coup", coup_hbm, coup),
+            ("near", near_hbm, near),
+            ("tbasis", tbasis_hbm, tbasis),
+            ("fk", fk_hbm, fk),
+            ("target", target_hbm, target),
+            ("owner", owner_hbm, owner),
+        )
+    ):
+        loads[name] = pltpu.make_async_copy(source, place, local_sem.at[k])
+        loads[name].start()
 
     pending = []
 
@@ -245,8 +274,11 @@
             tile=left,
         )
 
-    vb[0] = exc[...]
-    first_coeff = projected(exc[...], sbasis)
+    loads["exc"].wait()
+    loads["sbasis"].wait()
+    first_coeff = projected(vb[0], sbasis)
+    loads["rank"].wait()
+    loads["link"].wait()
 
     level = lax.broadcasted_iota(jnp.int32, (RANK, tiles), 0)
     source_tile = lax.broadcasted_iota(jnp.int32, (1, tiles), 1)
@@ -273,6 +305,7 @@
     gather(0, first_coeff, True)
     send_halo(0)
 
+    loads["coup"].wait()
     tile_row = lax.broadcasted_iota(jnp.int32, (tiles, group), 0)
     lane = lax.broadcasted_iota(jnp.int32, (tiles, group), 1)
     lane_row = lax.broadcasted_iota(jnp.int32, (1, group), 1)
@@ -283,17 +316,17 @@
         limit = dot(limit_rows, pick)
         position = (lane_row + to * group).astype(F32) - limit[PAIR : PAIR + 1, :] * float(RANK)
         keep = position < limit[:PAIR]
-        for c in range(2):
+        for c in range(2) if d == 0 else (core,):
             block = coup[c, :, aligned(to * group, group, 128)]
             block = jnp.where(keep, block.astype(F32), 0.0).astype(BF16)
             if d == 0:
                 mt[c, own_slice(q), :] = block
             else:
-                mt_send[d, c] = block
+                mt_send[d] = block
         if d != 0:
             send(
                 mt_send.at[d],
-                mt.at[:, own_slice(q), :],
+                mt.at[core, own_slice(q), :],
                 s_mt.at[d],
                 r_mt.at[d],
                 tile=q_peer(d),
@@ -323,17 +356,22 @@
             out = aligned(step * HALF, HALF, HALF)
             nacc[:, out] = nacc[:, out] + rows_joined(by_re, by_im)
 
-    near_copy.wait()
+    loads["near"].wait()
     for stage in range(2):
         if stage == 1:
             gather(1, projected(vb[1], sbasis), True)
             send_halo(1)
         near_own(stage)
+        if stage == 0:
+            for d in range(1, nq):
+                here = mt.at[core, own_slice(lax.rem(q + nq - d, nq)), :]
+                arrived(here, s_mt.at[d], r_mt.at[d])
+                send(here, here, s_sib.at[d], r_sib.at[d], src=sibling)
         gathered(stage, True)
         if stage == 0:
             for d in range(1, nq):
-                sender = lax.rem(q + nq - d, nq)
-                arrived(mt.at[:, own_slice(sender), :], s_mt.at[d], r_mt.at[d])
+                here = mt.at[1 - core, own_slice(lax.rem(q + nq - d, nq)), :]
+                arrived(here, s_sib.at[d], r_sib.at[d])
         coefficients = gath[stage, :group, :]
         scatter(
             stage,
@@ -346,25 +384,29 @@
         if stage == 0:
             for c in range(2):
                 mback[c] = jnp.transpose(mt[c].astype(F32)).astype(BF16)
+            loads["tbasis"].wait()
         coupled = scattered(stage, False)
         for l in range(2):
             cols = slice(l * TILE, (l + 1) * TILE)
             added = nacc[:, cols] + expanded(coupled, tbasis, l)
-            right_side = exc[:, cols].astype(F32)
+            right_side = vb[0, :, cols].astype(F32)
             if stage == 0:
                 value = right_side - DAMPING * added
             else:
-                before = field_out[:, cols]
+                before = field[:, cols]
                 value = before + DAMPING * (right_side - (before + added))
-            field_out[:, cols] = value
+            field[:, cols] = value
             vb[stage + 1, :, cols] = value.astype(BF16)
 
-    fk_copy.wait()
+    field_copy = pltpu.make_async_copy(field, field_out, local_sem.at[10])
+    field_copy.start()
+
+    loads["fk"].wait()
     x = vb[2]
-    fsend[...] = lanes_joined(dot_nt(fk[0], x), dot_nt(fk[1], x))
+    fsend[...] = lanes_joined(dot_nt(fk[0], x), dot_nt(fk[1], x)).astype(BF16)
 
     def f_rows(index):
-        return aligned(index * fgroup, fgroup, 8)
+        return aligned(index * fgroup, fgroup, 16)
 
     for d in far_order(nq):
         send(
@@ -374,10 +416,10 @@
             r_f.at[d],
             tile=q_peer(d),
         )
-    total = fsend[f_rows(q), :]
+    total = fsend[f_rows(q), :].astype(F32)
     for d in range(1, nq):
         arrived(fparts.at[d], s_f.at[d], r_f.at[d])
-        total = total + fparts[d]
+        total = total + fparts[d].astype(F32)
     fz[...] = total
 
     def z_rows(index):
@@ -398,31 +440,47 @@
     square = focal * focal
     strength = jnp.sum(square[:, :ROWS] + square[:, ROWS:], axis=1, keepdims=True)
     isum[...] = jnp.broadcast_to(strength, (8, 128))
-    for d in range(1, ns):
-        send(isum, iparts.at[d], s_i.at[d], r_i.at[d], src=lax.rem(s + d, ns))
-    slot = lax.broadcasted_iota(jnp.int32, (8, focal_count), 0)
-    spot = lax.broadcasted_iota(jnp.int32, (8, focal_count), 1)
+    fall[z_rows(z), :] = focal
+    for d in far_order(nz):
+        here = fall.at[z_rows(z)]
+        send(here, here, s_w.at[d], r_w.at[d], tile=z_peer(d))
+    others = [(e, d) for d in far_order(nz) + [0] for e in range(ns) if d or e]
+    for e, d in others:
+        send(
+            isum,
+            iparts.at[e, z_rows(z)],
+            s_i.at[e, d],
+            r_i.at[e, d],
+            tile=z_peer(d),
+            src=lax.rem(s + e, ns),
+        )
+    iparts[0, z_rows(z), :] = isum[...]
+    loads["target"].wait()
+    spot = lax.broadcasted_iota(jnp.int32, (fgroup, focal_count), 0)
+    wide = lax.broadcasted_iota(jnp.int32, (fgroup, focal_count), 1)
     wanted = jnp.sum(
-        jnp.where(spot == slot + t * 8, jnp.broadcast_to(target[...], (8, focal_count)), 0.0),
+        jnp.where(
+            wide == spot + q * fgroup,
+            jnp.broadcast_to(target[...], (fgroup, focal_count)),
+            0.0,
+        ),
         axis=1,
         keepdims=True,
     )
-    strength = isum[...]
-    for d in range(1, ns):
-        arrived(iparts.at[d], s_i.at[d], r_i.at[d])
-        strength = strength + iparts[d]
+    for e, d in others:
+        sender = lax.rem(z + nz - d, nz)
+        arrived(iparts.at[e, z_rows(sender)], s_i.at[e, d], r_i.at[e, d])
+    strength = iparts[0]
+    for e in range(1, ns):
+        strength = strength + iparts[e]
     residual = jnp.tanh(strength / (2.0 * ROWS * ns)) - wanted
-    wz[z_rows(z), :] = jnp.concatenate(
-        [residual * focal[:, :ROWS], -residual * focal[:, ROWS:], residual], axis=1
-    )
-    for d in far_order(nz):
-        here = wz.at[z_rows(z)]
-        send(here, here, s_w.at[d], r_w.at[d], tile=z_peer(d))
     for d in range(1, nz):
         sender = lax.rem(z + nz - d, nz)
-        arrived(wz.at[z_rows(sender)], s_w.at[d], r_w.at[d])
+        arrived(fall.at[z_rows(sender)], s_w.at[d], r_w.at[d])
     f16 = aligned(q * fgroup, fgroup, 16)
-    wg[f16, :] = wz[:, : 2 * ROWS].astype(BF16)
+    wg[f16, :] = jnp.concatenate(
+        [residual * fall[:, :ROWS], -residual * fall[:, ROWS:]], axis=1
+    ).astype(BF16)
     for d in far_order(nq):
         here = wg.at[f16]
         send(here, here, s_wg.at[d], r_wg.at[d], tile=q_peer(d))
@@ -430,7 +488,7 @@
     lane128 = lax.broadcasted_iota(jnp.int32, (fgroup, 128), 1)
     shift = lax.rem(q * fgroup, 128)
     flat = jnp.sum(
-        jnp.where(lane128 == row + shift, wz[:, 2 * ROWS :], 0.0), axis=0, keepdims=True
+        jnp.where(lane128 == row + shift, residual, 0.0), axis=0, keepdims=True
     )
     rrow[...] = jnp.broadcast_to(flat, (8, 128))
     rgath[q] = jnp.broadcast_to(flat, (8, 128))
@@ -448,7 +506,7 @@
         cols = aligned(step * HALF, HALF, HALF)
         w = wt[...]
         u = rows_joined(dot(w, fk[0, :, cols]), dot(w, fk[1, :, cols])) * scale
-        adj_out[:, cols] = u
+        adjoint[:, cols] = u
         vb[3, :, cols] = u.astype(BF16)
 
     gather(2, projected(vb[3], tbasis), False)
@@ -485,18 +543,25 @@
             by_im = by_im + dot_nt(x, near[i, m - i + 1, 1, half, :])
         nacc[:, aligned(step * HALF, HALF, HALF)] = rows_joined(by_re, by_im)
 
-    back = scattered(2, True)
     for side in range(2):
         arrived(edge_in.at[side], s_edge.at[side], r_edge.at[side])
+    back = scattered(2, True)
+    adjoint_copies = []
     for l in range(2):
         cols = slice(l * TILE, (l + 1) * TILE)
         added = nacc[:, cols] + edge_in[l].astype(F32) + expanded(back, sbasis, l)
-        adj_out[:, cols] = adj_out[:, cols] - DAMPING * added
+        adjoint[:, cols] = adjoint[:, cols] - DAMPING * added
+        copy = pltpu.make_async_copy(
+            adjoint.at[:, cols], adj_out.at[:, cols], local_sem.at[11 + l]
+        )
+        copy.start()
+        adjoint_copies.append(copy)
 
     lines = (focal_count + 127) // 128
     for d in range(1, nq):
         sender = lax.rem(q + nq - d, nq)
         arrived(rgath.at[sender], s_rr.at[d], r_rr.at[d])
+    loads["owner"].wait()
     mine = lax.broadcasted_iota(jnp.int32, (8, 128), 0) + t * 8
     found = jnp.zeros((8, 128), F32)
     for line in range(lines):
@@ -506,10 +571,30 @@
                 values = values + rgath[other]
         owners = jnp.broadcast_to(owner[line : line + 1, :], (8, 128))
         found = found + jnp.where(owners == mine, values, 0.0)
-    res_out[...] = jnp.broadcast_to(jnp.sum(found, axis=1, keepdims=True), (8, 128))
+    column = jnp.broadcast_to(jnp.sum(found, axis=1, keepdims=True), (8, 128))
+    diagonal = lax.broadcasted_iota(jnp.int32, (8, 128), 0) == lax.broadcasted_iota(
+        jnp.int32, (8, 128), 1
+    )
+    line = jnp.sum(jnp.where(diagonal, column, 0.0), axis=0, keepdims=True)
+    res_out[...] = line[:, :8]
 
     for copy in pending:
         copy.wait_send()
+    field_copy.wait()
+    for copy in adjoint_copies:
+        copy.wait()
+
+
+def hand_out(field, residual, adjoint, field_out, residual_out, adjoint_out, sem):
+    copies = [
+        pltpu.make_async_copy(field, field_out, sem.at[0]),
+        pltpu.make_async_copy(adjoint, adjoint_out, sem.at[1]),
+        pltpu.make_async_copy(residual, residual_out, sem.at[2]),
+    ]
+    for copy in copies:
+        copy.start()
+    for copy in copies:
+        copy.wait()
 
 
 def per_device(
@@ -544,37 +629,46 @@
         functools.partial(kernel, nz, nq, ns),
         out_shape=(
             jax.ShapeDtypeStruct((both, width), F32),
-            jax.ShapeDtypeStruct((8, 128), F32),
+            jax.ShapeDtypeStruct((1, 8), F32),
             jax.ShapeDtypeStruct((both, width), F32),
         ),
-        in_specs=[vmem, anywhere, vmem, vmem, vmem, vmem, vmem, anywhere, vmem, vmem],
-        out_specs=(vmem, vmem, vmem),
+        in_specs=[anywhere] * 10,
+        out_specs=(anywhere, vmem, anywhere),
         scratch_shapes=[
+            pltpu.VMEM((both, width), F32),
+            pltpu.VMEM((both, width), F32),
             pltpu.VMEM((2, 3, 2, TILE, TILE), BF16),
             pltpu.VMEM((2, focal_count, width), BF16),
+            pltpu.VMEM((2, PAIR, TILE), BF16),
+            pltpu.VMEM((2, PAIR, TILE), BF16),
+            pltpu.VMEM((2, PAIR, nq * group), BF16),
+            pltpu.VMEM((2, 2 * nt), jnp.int32),
+            pltpu.VMEM((2, 2 * nt), jnp.int32),
+            pltpu.VMEM((1, focal_count), F32),
+            pltpu.VMEM((lines, 128), jnp.int32),
             pltpu.VMEM((4, both, width), BF16),
             pltpu.VMEM((2, 2, both, TILE), BF16),
             pltpu.VMEM((both, width), F32),
-            pltpu.VMEM((nq, 2, PAIR, group), BF16),
+            pltpu.VMEM((nq, PAIR, group), BF16),
             pltpu.VMEM((2, spread, group), BF16),
             pltpu.VMEM((2, group, spread), BF16),
             pltpu.VMEM((3, most * PAIR, both), BF16),
             pltpu.VMEM((3, most * PAIR, both), BF16),
             pltpu.VMEM((3, most, PAIR, both), BF16),
-            pltpu.VMEM((focal_count, both), F32),
-            pltpu.VMEM((nq, fgroup, both), F32),
+            pltpu.VMEM((focal_count, both), BF16),
+            pltpu.VMEM((nq, fgroup, both), BF16),
             pltpu.VMEM((fgroup, both), F32),
             pltpu.VMEM((nz, 8, both), F32),
             pltpu.VMEM((8, 128), F32),
-            pltpu.VMEM((ns, 8, 128), F32),
-            pltpu.VMEM((fgroup, 3 * ROWS), F32),
+            pltpu.VMEM((ns, fgroup, 128), F32),
+            pltpu.VMEM((fgroup, both), F32),
             pltpu.VMEM((focal_count, both), BF16),
             pltpu.VMEM((both, focal_count), BF16),
             pltpu.VMEM((8, 128), F32),
             pltpu.VMEM((nq, 8, 128), F32),
             pltpu.VMEM((2, both, TILE), BF16),
             pltpu.VMEM((2, both, TILE), BF16),
-            dma((2,)),
+            dma((13,)),
             dma((2, 2)),
             dma((2, 2)),
             dma((nq,)),
@@ -587,10 +681,12 @@
             dma((nq,)),
             dma((nz,)),
             dma((nz,)),
-            dma((ns,)),
-            dma((ns,)),
+            dma((ns, nz)),
+            dma((ns, nz)),
             dma((nz,)),
             dma((nz,)),
+            dma((nq,)),
+            dma((nq,)),
             dma((nq,)),
             dma((nq,)),
             dma((nq,)),
@@ -599,7 +695,7 @@
             dma((2,)),
         ],
         compiler_params=pltpu.CompilerParams(
-            collective_id=0, has_side_effects=True, vmem_limit_bytes=48 * 1024 * 1024
+            collective_id=0, has_side_effects=True, vmem_limit_bytes=56 * 1024 * 1024
         ),
     )(
         excitation.reshape(both, width),
@@ -613,9 +709,20 @@
         focal_target.reshape(1, focal_count),
         owner.reshape(lines, 128),
     )
+    field, residual, adjoint = pl.pallas_call(
+        hand_out,
+        out_shape=(
+            jax.ShapeDtypeStruct((both, width), F32),
+            jax.ShapeDtypeStruct((1, 8), F32),
+            jax.ShapeDtypeStruct((both, width), F32),
+        ),
+        in_specs=[anywhere] * 3,
+        out_specs=[anywhere] * 3,
+        scratch_shapes=[dma((3,))],
+    )(field, residual, adjoint)
     return (
         field.reshape(2, ROWS, width),
-        residual[:, 0],
+        residual.reshape(8),
         adjoint.reshape(2, ROWS, width),
     )
 

time: 96.9 us -> 149 us (1.54)
  Pallas kernels: 85.2 us -> 148 us
  local copies, waits for them, and re-layouts: 10.8 us -> 0 us
    pallas_call x0 -> x1, Pallas kernels: none -> 64.7 us  [per_device(): pl.pallas_call(hand_out, out_shape=(jax.ShapeDtypeStruct((both, width), F...]
    unnamed x20 -> x0, local copies, waits for them, and re-layouts: 10.1 us -> none
    pallas_call x1, Pallas kernels: 85.2 us -> 83.6 us  [per_device(): pl.pallas_call(functools.partial(kernel, nz, nq, ns), out_shape=(jax.Shap...]
where the time goes in v2:
time: 149 us
  Pallas kernels  148 us (99%)
    pallas_call x1, Pallas kernels, per_device(): pl.pallas_call(functools.partial(kernel, nz, nq, ns), out_shape=(jax.Shap...  83.6 us
    pallas_call x1, Pallas kernels, per_device(): pl.pallas_call(hand_out, out_shape=(jax.ShapeDtypeStruct((both, width), F...  64.7 us

profile of v2, /device:TPU:2, one launch (start us, length us, event | category | flops | bytes accessed | tf_op | source)
XLA Modules:
  0.0 148.9 jit_solution(6001498229833111812)
XLA Ops:
  0.6 83.6 %shard_map.121 = (f32[256,1024]{1,0:T(8,128)}, f32[1,8]{1,0:T(1,128)}, f32[256,1024]{1,0:T(8,128)}) custom-call(bf16[256,1024]{1,0:T(8,128)(2,1)} %bitcast.12, bf16[2,3,2,512,512]{4,3,2,1,0:T(8,128)(2,1)} %near_hbm.1, bf16[2,48,512]{2,1,0:T(8,128)(2,1)} %bitcast.13, bf16[2,48,512]{2,1,0:T(8,128)(2,1)} %bitcast.14, bf16[2,48,3072]{2,1,0:T(8,128)(2,1)} %bitcast.11, ...), custom_call_target="tpu_custom_call" | custom-call | tf_op jit(solution)/shard_map/pallas_call | solution.py:628
  84.2 64.7 %shard_map.122 = (f32[256,1024]{1,0:T(8,128)}, f32[1,8]{1,0:T(1,128)}, f32[256,1024]{1,0:T(8,128)}) custom-call(f32[256,1024]{1,0:T(8,128)} %get-tuple-element.9.field, f32[1,8]{1,0:T(1,128)} %get-tuple-element.10.residual, f32[256,1024]{1,0:T(8,128)} %get-tuple-element.11.adjoint), custom_call_target="tpu_custom_call" | custom-call | tf_op jit(solution)/shard_map/pallas_call | solution.py:712

commit v3 on v2

--- a/solution.py
+++ b/solution.py
@@ -84,7 +84,6 @@
     fzparts,
     isum,
     iparts,
-    fall,
     wg,
     wt,
     rrow,
@@ -106,8 +105,6 @@
     r_fz,
     s_i,
     r_i,
-    s_w,
-    r_w,
     s_sib,
     r_sib,
     s_wg,
@@ -145,15 +142,12 @@
     for other in (left, right):
         pl.semaphore_signal(barrier, inc=1, device_id={"tile": other, "src": s})
         count += 1
-    for e in range(ns):
-        for d in range(nz):
-            if d or e:
-                pl.semaphore_signal(
-                    barrier,
-                    inc=1,
-                    device_id={"tile": z_peer(d), "src": lax.rem(s + e, ns)},
-                )
-                count += 1
+    for d in range(1, nz):
+        pl.semaphore_signal(barrier, inc=1, device_id={"tile": z_peer(d), "src": s})
+        count += 1
+    for e in range(1, ns):
+        pl.semaphore_signal(barrier, inc=1, device_id={"tile": t, "src": lax.rem(s + e, ns)})
+        count += 1
     core = lax.rem(s, 2)
     sibling = s + 1 - 2 * core
 
@@ -420,76 +414,40 @@
     for d in range(1, nq):
         arrived(fparts.at[d], s_f.at[d], r_f.at[d])
         total = total + fparts[d].astype(F32)
-    fz[...] = total
-
-    def z_rows(index):
-        return aligned(index * 8, 8, 8)
-
+    fz[...] = total.astype(BF16)
     for d in far_order(nz):
-        send(
-            fz.at[z_rows(lax.rem(z + d, nz))],
-            fzparts.at[d],
-            s_fz.at[d],
-            r_fz.at[d],
-            tile=z_peer(d),
-        )
-    focal = fz[z_rows(z), :]
+        send(fz, fzparts.at[d], s_fz.at[d], r_fz.at[d], tile=z_peer(d))
+    row = lax.broadcasted_iota(jnp.int32, (fgroup, 128), 0)
+    lane128 = lax.broadcasted_iota(jnp.int32, (fgroup, 128), 1)
+    shift = lax.rem(q * fgroup, 128)
+    diagonal = lane128 == row + shift
+    loads["target"].wait()
+    wanted = target[pl.ds(q * fgroup // 128, 1), :]
+    focal = fz[...].astype(F32)
     for d in range(1, nz):
         arrived(fzparts.at[d], s_fz.at[d], r_fz.at[d])
-        focal = focal + fzparts[d]
+        focal = focal + fzparts[d].astype(F32)
     square = focal * focal
     strength = jnp.sum(square[:, :ROWS] + square[:, ROWS:], axis=1, keepdims=True)
-    isum[...] = jnp.broadcast_to(strength, (8, 128))
-    fall[z_rows(z), :] = focal
-    for d in far_order(nz):
-        here = fall.at[z_rows(z)]
-        send(here, here, s_w.at[d], r_w.at[d], tile=z_peer(d))
-    others = [(e, d) for d in far_order(nz) + [0] for e in range(ns) if d or e]
-    for e, d in others:
-        send(
-            isum,
-            iparts.at[e, z_rows(z)],
-            s_i.at[e, d],
-            r_i.at[e, d],
-            tile=z_peer(d),
-            src=lax.rem(s + e, ns),
-        )
-    iparts[0, z_rows(z), :] = isum[...]
-    loads["target"].wait()
-    spot = lax.broadcasted_iota(jnp.int32, (fgroup, focal_count), 0)
-    wide = lax.broadcasted_iota(jnp.int32, (fgroup, focal_count), 1)
-    wanted = jnp.sum(
-        jnp.where(
-            wide == spot + q * fgroup,
-            jnp.broadcast_to(target[...], (fgroup, focal_count)),
-            0.0,
-        ),
-        axis=1,
-        keepdims=True,
-    )
-    for e, d in others:
-        sender = lax.rem(z + nz - d, nz)
-        arrived(iparts.at[e, z_rows(sender)], s_i.at[e, d], r_i.at[e, d])
-    strength = iparts[0]
+    line = jnp.sum(jnp.where(diagonal, strength, 0.0), axis=0, keepdims=True)
+    isum[...] = jnp.broadcast_to(line, (8, 128))
+    for e in far_order(ns):
+        send(isum, iparts.at[e], s_i.at[e], r_i.at[e], src=lax.rem(s + e, ns))
+    strength = line
     for e in range(1, ns):
-        strength = strength + iparts[e]
-    residual = jnp.tanh(strength / (2.0 * ROWS * ns)) - wanted
-    for d in range(1, nz):
-        sender = lax.rem(z + nz - d, nz)
-        arrived(fall.at[z_rows(sender)], s_w.at[d], r_w.at[d])
+        arrived(iparts.at[e], s_i.at[e], r_i.at[e])
+        strength = strength + iparts[e, :1, :]
+    in_line = lane128[:1] - shift
+    in_line = (in_line >= 0) & (in_line < fgroup)
+    flat = jnp.where(in_line, jnp.tanh(strength / (2.0 * ROWS * ns)) - wanted, 0.0)
+    residual = jnp.sum(jnp.where(diagonal, flat, 0.0), axis=1, keepdims=True)
     f16 = aligned(q * fgroup, fgroup, 16)
     wg[f16, :] = jnp.concatenate(
-        [residual * fall[:, :ROWS], -residual * fall[:, ROWS:]], axis=1
+        [residual * focal[:, :ROWS], -residual * focal[:, ROWS:]], axis=1
     ).astype(BF16)
     for d in far_order(nq):
         here = wg.at[f16]
         send(here, here, s_wg.at[d], r_wg.at[d], tile=q_peer(d))
-    row = lax.broadcasted_iota(jnp.int32, (fgroup, 128), 0)
-    lane128 = lax.broadcasted_iota(jnp.int32, (fgroup, 128), 1)
-    shift = lax.rem(q * fgroup, 128)
-    flat = jnp.sum(
-        jnp.where(lane128 == row + shift, residual, 0.0), axis=0, keepdims=True
-    )
     rrow[...] = jnp.broadcast_to(flat, (8, 128))
     rgath[q] = jnp.broadcast_to(flat, (8, 128))
     for d in far_order(nq):
@@ -585,16 +543,26 @@
         copy.wait()
 
 
-def hand_out(field, residual, adjoint, field_out, residual_out, adjoint_out, sem):
-    copies = [
-        pltpu.make_async_copy(field, field_out, sem.at[0]),
-        pltpu.make_async_copy(adjoint, adjoint_out, sem.at[1]),
-        pltpu.make_async_copy(residual, residual_out, sem.at[2]),
-    ]
-    for copy in copies:
+CHUNKS = 4
+
+
+def hand_out(field, residual, adjoint, field_out, residual_out, adjoint_out, held, in_sem, out_sem):
+    residual_out[...] = residual[...]
+    rows = held.shape[1] // CHUNKS
+    loads, stores = [], []
+    for k, (source, target) in enumerate(((field, field_out), (adjoint, adjoint_out))):
+        for c in range(CHUNKS):
+            part = pl.ds(c * rows, rows)
+            here = held.at[k, part]
+            loads.append(pltpu.make_async_copy(source.at[part], here, in_sem.at[k, c]))
+            stores.append(pltpu.make_async_copy(here, target.at[part], out_sem.at[k, c]))
+    for copy in loads:
         copy.start()
-    for copy in copies:
-        copy.wait()
+    for load, store in zip(loads, stores):
+        load.wait()
+        store.start()
+    for store in stores:
+        store.wait()
 
 
 def per_device(
@@ -620,6 +588,7 @@
     width = 2 * TILE
     most = max(nz, nq)
     lines = (focal_count + 127) // 128
+    wanted = jnp.pad(focal_target, (0, lines * 128 - focal_count))
     owner = jnp.pad(focal_owner, (0, lines * 128 - focal_count), constant_values=-1)
     vmem = pl.BlockSpec(memory_space=pltpu.VMEM)
     anywhere = pl.BlockSpec(memory_space=pl.ANY)
@@ -644,7 +613,7 @@
             pltpu.VMEM((2, PAIR, nq * group), BF16),
             pltpu.VMEM((2, 2 * nt), jnp.int32),
             pltpu.VMEM((2, 2 * nt), jnp.int32),
-            pltpu.VMEM((1, focal_count), F32),
+            pltpu.VMEM((lines, 128), F32),
             pltpu.VMEM((lines, 128), jnp.int32),
             pltpu.VMEM((4, both, width), BF16),
             pltpu.VMEM((2, 2, both, TILE), BF16),
@@ -657,11 +626,10 @@
             pltpu.VMEM((3, most, PAIR, both), BF16),
             pltpu.VMEM((focal_count, both), BF16),
             pltpu.VMEM((nq, fgroup, both), BF16),
-            pltpu.VMEM((fgroup, both), F32),
-            pltpu.VMEM((nz, 8, both), F32),
+            pltpu.VMEM((fgroup, both), BF16),
+            pltpu.VMEM((nz, fgroup, both), BF16),
             pltpu.VMEM((8, 128), F32),
-            pltpu.VMEM((ns, fgroup, 128), F32),
-            pltpu.VMEM((fgroup, both), F32),
+            pltpu.VMEM((ns, 8, 128), F32),
             pltpu.VMEM((focal_count, both), BF16),
             pltpu.VMEM((both, focal_count), BF16),
             pltpu.VMEM((8, 128), F32),
@@ -681,10 +649,8 @@
             dma((nq,)),
             dma((nz,)),
             dma((nz,)),
-            dma((ns, nz)),
-            dma((ns, nz)),
-            dma((nz,)),
-            dma((nz,)),
+            dma((ns,)),
+            dma((ns,)),
             dma((nq,)),
             dma((nq,)),
             dma((nq,)),
@@ -706,7 +672,7 @@
         pair_rank.T,
         far_link.T,
         focal_kernel,
-        focal_target.reshape(1, focal_count),
+        wanted.reshape(lines, 128),
         owner.reshape(lines, 128),
     )
     field, residual, adjoint = pl.pallas_call(
@@ -716,9 +682,14 @@
             jax.ShapeDtypeStruct((1, 8), F32),
             jax.ShapeDtypeStruct((both, width), F32),
         ),
-        in_specs=[anywhere] * 3,
-        out_specs=[anywhere] * 3,
-        scratch_shapes=[dma((3,))],
+        in_specs=[anywhere, vmem, anywhere],
+        out_specs=[anywhere, vmem, anywhere],
+        scratch_shapes=[
+            pltpu.VMEM((2, both, width), F32),
+            dma((2, CHUNKS)),
+            dma((2, CHUNKS)),
+        ],
+        compiler_params=pltpu.CompilerParams(vmem_limit_bytes=56 * 1024 * 1024),
     )(field, residual, adjoint)
     return (
         field.reshape(2, ROWS, width),

time: 149 us -> 83.8 us (0.56)
  Pallas kernels: 148 us -> 82.5 us
    pallas_call x1, Pallas kernels: 64.7 us -> 3.51 us  [per_device(): pl.pallas_call(hand_out, out_shape=(jax.ShapeDtypeStruct((both, width), F...]
    pallas_call x1, Pallas kernels: 83.6 us -> 79 us  [per_device(): pl.pallas_call(functools.partial(kernel, nz, nq, ns), out_shape=(jax.Shap...]
where the time goes in v3:
time: 83.8 us; the launch traced here: 83.2 us
  Pallas kernels  82.5 us (98%)
    pallas_call x1, Pallas kernels, per_device(): pl.pallas_call(functools.partial(kernel, nz, nq, ns), out_shape=(jax.Shap...  79 us
    pallas_call x1, Pallas kernels, per_device(): pl.pallas_call(hand_out, out_shape=(jax.ShapeDtypeStruct((both, width), F...  3.51 us

profile of v3, /device:TPU:2, one launch (start us, length us, event | category | flops | bytes accessed | tf_op | source)
XLA Modules:
  0.0 83.2 jit_solution(7736942209446124728)
XLA Ops:
  0.6 79.0 %shard_map.121 = (f32[256,1024]{1,0:T(8,128)}, f32[1,8]{1,0:T(1,128)}, f32[256,1024]{1,0:T(8,128)}) custom-call(bf16[256,1024]{1,0:T(8,128)(2,1)} %bitcast.12, bf16[2,3,2,512,512]{4,3,2,1,0:T(8,128)(2,1)} %near_hbm.1, bf16[2,48,512]{2,1,0:T(8,128)(2,1)} %bitcast.13, bf16[2,48,512]{2,1,0:T(8,128)(2,1)} %bitcast.14, bf16[2,48,3072]{2,1,0:T(8,128)(2,1)} %bitcast.11, ...), custom_call_target="tpu_custom_call" | custom-call | tf_op jit(solution)/shard_map/pallas_call | solution.py:597
  79.7 3.5 %shard_map.122 = (f32[256,1024]{1,0:T(8,128)}, f32[1,8]{1,0:T(1,128)}, f32[256,1024]{1,0:T(8,128)}) custom-call(f32[256,1024]{1,0:T(8,128)} %get-tuple-element.9.field, f32[1,8]{1,0:T(1,128)} %get-tuple-element.10.residual, f32[256,1024]{1,0:T(8,128)} %get-tuple-element.11.adjoint), custom_call_target="tpu_custom_call" | custom-call | tf_op jit(solution)/shard_map/pallas_call | solution.py:678

commit v4 on v3

--- a/solution.py
+++ b/solution.py
@@ -26,15 +26,29 @@
 
 
 def rows_joined(by_re, by_im):
-    return jnp.concatenate(
-        [by_re[:ROWS] - by_im[ROWS:], by_re[ROWS:] + by_im[:ROWS]], axis=0
-    )
+    shape = by_re.shape
+    blocks = (shape[0] // ROWS, 2, ROWS // 2, shape[1])
+    by_re, by_im = by_re.reshape(blocks), by_im.reshape(blocks)
+    re = by_re[:, 0] - by_im[:, 1]
+    im = by_re[:, 1] + by_im[:, 0]
+    return jnp.stack([re, im], axis=1).reshape(shape)
+
+
+def turned(x):
+    lane = lax.broadcasted_iota(jnp.int32, (1, ROWS), 1)
+    sign = jnp.where(lane < ROWS // 2, -1.0, 1.0)
+    blocks = [
+        pltpu.roll(x[:, k : k + ROWS], ROWS // 2, 1) * sign for k in range(0, x.shape[1], ROWS)
+    ]
+    return blocks[0] if len(blocks) == 1 else jnp.concatenate(blocks, axis=1)
 
 
 def lanes_joined(by_re, by_im):
-    return jnp.concatenate(
-        [by_re[:, :ROWS] - by_im[:, ROWS:], by_re[:, ROWS:] + by_im[:, :ROWS]], axis=1
-    )
+    return by_re + turned(by_im)
+
+
+def half_of(h):
+    return slice(0, 2 * ROWS) if h is None else slice(h * ROWS, (h + 1) * ROWS)
 
 
 def aligned(start, size, unit):
@@ -151,10 +165,19 @@
     core = lax.rem(s, 2)
     sibling = s + 1 - 2 * core
 
+    half = ROWS // 2
     loads = {}
     for k, (name, source, place) in enumerate(
         (
-            ("exc", exc_hbm, vb.at[0]),
+            *(
+                (
+                    ("exc", h, c),
+                    exc_hbm.at[c, h * half : (h + 1) * half],
+                    vb.at[0, (2 * h + c) * half : (2 * h + c + 1) * half],
+                )
+                for h in range(2)
+                for c in range(2)
+            ),
             ("sbasis", sbasis_hbm, sbasis),
             ("rank", rank_hbm, rank),
             ("link", link_hbm, link),
@@ -204,71 +227,83 @@
             pieces.append(lanes_joined(both[:RANK], both[RANK:]))
         return jnp.concatenate(pieces, axis=0).astype(BF16)
 
-    def gather(stage, value, along_z):
+    def gather(stage, h, value, along_z):
         n, mine = (nz, z) if along_z else (nq, q)
-        here = gath.at[stage, own_slice(mine)]
-        gath[stage, own_slice(mine), :] = value
+        lanes = half_of(h)
+        here = gath.at[stage, own_slice(mine), lanes]
+        gath[stage, own_slice(mine), lanes] = value
         for d in far_order(n):
             send(
                 here,
                 here,
-                s_gath.at[stage, d],
-                r_gath.at[stage, d],
+                s_gath.at[stage, h or 0, d],
+                r_gath.at[stage, h or 0, d],
                 tile=z_peer(d) if along_z else q_peer(d),
             )
 
-    def gathered(stage, along_z):
+    def gathered(stage, h, along_z):
         n, mine = (nz, z) if along_z else (nq, q)
         for d in range(1, n):
             sender = lax.rem(mine + n - d, n)
             arrived(
-                gath.at[stage, own_slice(sender)], s_gath.at[stage, d], r_gath.at[stage, d]
-            )
-
-    def scatter(stage, value, along_z):
+                gath.at[stage, own_slice(sender), half_of(h)],
+                s_gath.at[stage, h or 0, d],
+                r_gath.at[stage, h or 0, d],
+            )
+        return gath[stage, : n * PAIR, half_of(h)]
+
+    def scatter(stage, h, value, along_z):
         n, mine = (nz, z) if along_z else (nq, q)
-        part[stage] = value.astype(BF16)
+        lanes = half_of(h)
+        part[stage, :, lanes] = value.astype(BF16)
         for d in far_order(n):
             owner_of = lax.rem(mine + d, n)
             send(
-                part.at[stage, own_slice(owner_of)],
-                parts_in.at[stage, d],
-                s_part.at[stage, d],
-                r_part.at[stage, d],
+                part.at[stage, own_slice(owner_of), lanes],
+                parts_in.at[stage, d, :, lanes],
+                s_part.at[stage, h or 0, d],
+                r_part.at[stage, h or 0, d],
                 tile=z_peer(d) if along_z else q_peer(d),
             )
 
-    def scattered(stage, along_z):
+    def scattered(stage, h, along_z):
         n, mine = (nz, z) if along_z else (nq, q)
-        total = part[stage, own_slice(mine), :].astype(F32)
+        lanes = half_of(h)
+        total = part[stage, own_slice(mine), lanes].astype(F32)
         for d in range(1, n):
-            arrived(parts_in.at[stage, d], s_part.at[stage, d], r_part.at[stage, d])
-            total = total + parts_in[stage, d].astype(F32)
+            arrived(
+                parts_in.at[stage, d, :, lanes],
+                s_part.at[stage, h or 0, d],
+                r_part.at[stage, h or 0, d],
+            )
+            total = total + parts_in[stage, d, :, lanes].astype(F32)
         return total.astype(BF16).astype(F32)
 
     def expanded(coefficients, basis, l):
         piece = coefficients[l * RANK : (l + 1) * RANK]
-        turned = jnp.concatenate([-piece[:, ROWS:], piece[:, :ROWS]], axis=1)
-        stacked = jnp.concatenate([piece, turned], axis=0)
+        stacked = jnp.concatenate([piece, turned(piece)], axis=0)
         return dot(jnp.transpose(stacked).astype(BF16), basis[l])
 
-    def send_halo(stage):
+    def send_halo(stage, h):
+        rows = half_of(h)
         send(
-            vb.at[stage, :, TILE : 2 * TILE],
-            halo.at[stage, 0],
-            s_halo.at[stage, 0],
-            r_halo.at[stage, 0],
+            vb.at[stage, rows, TILE : 2 * TILE],
+            halo.at[stage, 0, rows],
+            s_halo.at[stage, h, 0],
+            r_halo.at[stage, h, 0],
             tile=right,
         )
         send(
-            vb.at[stage, :, 0:TILE],
-            halo.at[stage, 1],
-            s_halo.at[stage, 1],
-            r_halo.at[stage, 1],
+            vb.at[stage, rows, 0:TILE],
+            halo.at[stage, 1, rows],
+            s_halo.at[stage, h, 1],
+            r_halo.at[stage, h, 1],
             tile=left,
         )
 
-    loads["exc"].wait()
+    for h in range(2):
+        for c in range(2):
+            loads["exc", h, c].wait()
     loads["sbasis"].wait()
     first_coeff = projected(vb[0], sbasis)
     loads["rank"].wait()
@@ -296,8 +331,9 @@
 
     pl.semaphore_wait(barrier, count)
 
-    gather(0, first_coeff, True)
-    send_halo(0)
+    for h in range(2):
+        gather(0, h, first_coeff[:, half_of(h)], True)
+        send_halo(0, h)
 
     loads["coup"].wait()
     tile_row = lax.broadcasted_iota(jnp.int32, (tiles, group), 0)
@@ -326,97 +362,124 @@
                 tile=q_peer(d),
             )
 
-    def near_own(stage):
+    def near_own(stage, h):
+        rows = half_of(h)
+
         @pl.loop(0, 4)
         def _(step):
             i = step // 2
             cols = aligned((step % 2) * HALF, HALF, HALF)
-            by_re = jnp.zeros((2 * ROWS, HALF), F32)
-            by_im = jnp.zeros((2 * ROWS, HALF), F32)
+            by_re = by_im = 0.0
             for l in range(2):
-                x = vb[stage, :, l * TILE : (l + 1) * TILE]
+                x = vb[stage, rows, l * TILE : (l + 1) * TILE]
                 by_re = by_re + dot(x, near[i, l - i + 1, 0, :, cols])
                 by_im = by_im + dot(x, near[i, l - i + 1, 1, :, cols])
-            nacc[:, aligned(step * HALF, HALF, HALF)] = rows_joined(by_re, by_im)
-
-    def near_halo(stage):
+            nacc[rows, aligned(step * HALF, HALF, HALF)] = rows_joined(by_re, by_im)
+
+    def near_halo(stage, h):
+        rows = half_of(h)
+        for side in range(2):
+            arrived(
+                halo.at[stage, side, rows],
+                s_halo.at[stage, h, side],
+                r_halo.at[stage, h, side],
+            )
+
         @pl.loop(0, 4)
         def _(step):
             i = step // 2
             cols = aligned((step % 2) * HALF, HALF, HALF)
-            x = halo[stage, i]
+            x = halo[stage, i, rows]
             by_re = dot(x, near[i, 2 * i, 0, :, cols])
             by_im = dot(x, near[i, 2 * i, 1, :, cols])
             out = aligned(step * HALF, HALF, HALF)
-            nacc[:, out] = nacc[:, out] + rows_joined(by_re, by_im)
-
-    loads["near"].wait()
-    for stage in range(2):
-        if stage == 1:
-            gather(1, projected(vb[1], sbasis), True)
-            send_halo(1)
-        near_own(stage)
-        if stage == 0:
-            for d in range(1, nq):
-                here = mt.at[core, own_slice(lax.rem(q + nq - d, nq)), :]
-                arrived(here, s_mt.at[d], r_mt.at[d])
-                send(here, here, s_sib.at[d], r_sib.at[d], src=sibling)
-        gathered(stage, True)
-        if stage == 0:
-            for d in range(1, nq):
-                here = mt.at[1 - core, own_slice(lax.rem(q + nq - d, nq)), :]
-                arrived(here, s_sib.at[d], r_sib.at[d])
-        coefficients = gath[stage, :group, :]
+            nacc[rows, out] = nacc[rows, out] + rows_joined(by_re, by_im)
+
+    def couple(stage, h):
+        coefficients = gathered(stage, h, True)
         scatter(
-            stage,
-            lanes_joined(dot(mt[0], coefficients), dot(mt[1], coefficients)),
-            False,
+            stage, h, lanes_joined(dot(mt[0], coefficients), dot(mt[1], coefficients)), False
         )
-        for side in range(2):
-            arrived(halo.at[stage, side], s_halo.at[stage, side], r_halo.at[stage, side])
-        near_halo(stage)
-        if stage == 0:
-            for c in range(2):
-                mback[c] = jnp.transpose(mt[c].astype(F32)).astype(BF16)
-            loads["tbasis"].wait()
-        coupled = scattered(stage, False)
+
+    def updated(stage, h):
+        near_halo(stage, h)
+        coupled = scattered(stage, h, False)
+        rows = half_of(h)
         for l in range(2):
             cols = slice(l * TILE, (l + 1) * TILE)
-            added = nacc[:, cols] + expanded(coupled, tbasis, l)
-            right_side = vb[0, :, cols].astype(F32)
+            added = nacc[rows, cols] + expanded(coupled, tbasis, l)
+            right_side = vb[0, rows, cols].astype(F32)
             if stage == 0:
                 value = right_side - DAMPING * added
             else:
-                before = field[:, cols]
+                before = field[rows, cols]
                 value = before + DAMPING * (right_side - (before + added))
-            field[:, cols] = value
-            vb[stage + 1, :, cols] = value.astype(BF16)
-
-    field_copy = pltpu.make_async_copy(field, field_out, local_sem.at[10])
-    field_copy.start()
-
+            field[rows, cols] = value
+            vb[stage + 1, rows, cols] = value.astype(BF16)
+
+    loads["near"].wait()
+    near_own(0, None)
+    for d in range(1, nq):
+        here = mt.at[core, own_slice(lax.rem(q + nq - d, nq)), :]
+        arrived(here, s_mt.at[d], r_mt.at[d])
+        send(here, here, s_sib.at[d], r_sib.at[d], src=sibling)
+    for d in range(1, nq):
+        here = mt.at[1 - core, own_slice(lax.rem(q + nq - d, nq)), :]
+        arrived(here, s_sib.at[d], r_sib.at[d])
+    for h in range(2):
+        couple(0, h)
+    for c in range(2):
+        mback[c] = jnp.transpose(mt[c].astype(F32)).astype(BF16)
+    loads["tbasis"].wait()
+    for h in range(2):
+        updated(0, h)
+        gather(1, h, projected(vb[1, half_of(h)], sbasis), True)
+        send_halo(1, h)
+    for h in range(2):
+        near_own(1, h)
+        couple(1, h)
     loads["fk"].wait()
-    x = vb[2]
-    fsend[...] = lanes_joined(dot_nt(fk[0], x), dot_nt(fk[1], x)).astype(BF16)
+    copies = []
 
     def f_rows(index):
         return aligned(index * fgroup, fgroup, 16)
 
-    for d in far_order(nq):
-        send(
-            fsend.at[f_rows(lax.rem(q + d, nq))],
-            fparts.at[d],
-            s_f.at[d],
-            r_f.at[d],
-            tile=q_peer(d),
-        )
-    total = fsend[f_rows(q), :].astype(F32)
-    for d in range(1, nq):
-        arrived(fparts.at[d], s_f.at[d], r_f.at[d])
-        total = total + fparts[d].astype(F32)
-    fz[...] = total.astype(BF16)
-    for d in far_order(nz):
-        send(fz, fzparts.at[d], s_fz.at[d], r_fz.at[d], tile=z_peer(d))
+    for h in range(2):
+        updated(1, h)
+        for c in range(2):
+            copy = pltpu.make_async_copy(
+                field.at[(2 * h + c) * half : (2 * h + c + 1) * half],
+                field_out.at[c, h * half : (h + 1) * half],
+                local_sem.at[13 + 2 * h + c],
+            )
+            copy.start()
+            copies.append(copy)
+        lanes = half_of(h)
+        x = vb[2, lanes]
+        fsend[:, lanes] = lanes_joined(dot_nt(fk[0], x), dot_nt(fk[1], x)).astype(BF16)
+        for d in far_order(nq):
+            send(
+                fsend.at[f_rows(lax.rem(q + d, nq)), lanes],
+                fparts.at[d, :, lanes],
+                s_f.at[h, d],
+                r_f.at[h, d],
+                tile=q_peer(d),
+            )
+    for h in range(2):
+        lanes = half_of(h)
+        total = fsend[f_rows(q), lanes].astype(F32)
+        for d in range(1, nq):
+            arrived(fparts.at[d, :, lanes], s_f.at[h, d], r_f.at[h, d])
+            total = total + fparts[d, :, lanes].astype(F32)
+        fz[:, lanes] = total.astype(BF16)
+        for d in far_order(nz):
+            send(
+                fz.at[:, lanes],
+                fzparts.at[d, :, lanes],
+                s_fz.at[h, d],
+                r_fz.at[h, d],
+                tile=z_peer(d),
+            )
     row = lax.broadcasted_iota(jnp.int32, (fgroup, 128), 0)
     lane128 = lax.broadcasted_iota(jnp.int32, (fgroup, 128), 1)
     shift = lax.rem(q * fgroup, 128)
@@ -425,7 +488,8 @@
     wanted = target[pl.ds(q * fgroup // 128, 1), :]
     focal = fz[...].astype(F32)
     for d in range(1, nz):
-        arrived(fzparts.at[d], s_fz.at[d], r_fz.at[d])
+        for h in range(2):
+            arrived(fzparts.at[d, :, half_of(h)], s_fz.at[h, d], r_fz.at[h, d])
         focal = focal + fzparts[d].astype(F32)
     square = focal * focal
     strength = jnp.sum(square[:, :ROWS] + square[:, ROWS:], axis=1, keepdims=True)
@@ -442,9 +506,9 @@
     flat = jnp.where(in_line, jnp.tanh(strength / (2.0 * ROWS * ns)) - wanted, 0.0)
     residual = jnp.sum(jnp.where(diagonal, flat, 0.0), axis=1, keepdims=True)
     f16 = aligned(q * fgroup, fgroup, 16)
-    wg[f16, :] = jnp.concatenate(
-        [residual * focal[:, :ROWS], -residual * focal[:, ROWS:]], axis=1
-    ).astype(BF16)
+    sign = jnp.where(lane128[:1] < ROWS // 2, 1.0, -1.0)
+    sign = jnp.concatenate([sign, sign], axis=1)
+    wg[f16, :] = (residual * focal * sign).astype(BF16)
     for d in far_order(nq):
         here = wg.at[f16]
         send(here, here, s_wg.at[d], r_wg.at[d], tile=q_peer(d))
@@ -467,7 +531,7 @@
         adjoint[:, cols] = u
         vb[3, :, cols] = u.astype(BF16)
 
-    gather(2, projected(vb[3], tbasis), False)
+    gather(2, None, projected(vb[3], tbasis), False)
 
     @pl.loop(0, 4)
     def _(step):
@@ -481,10 +545,10 @@
     send(edge_send.at[0], edge_in.at[1], s_edge.at[0], r_edge.at[1], tile=left)
     send(edge_send.at[1], edge_in.at[0], s_edge.at[1], r_edge.at[0], tile=right)
 
-    gathered(2, False)
-    coefficients = gath[2, :spread, :]
+    coefficients = gathered(2, None, False)
     scatter(
         2,
+        None,
         lanes_joined(dot(mback[0], coefficients), dot(mback[1], coefficients)),
         True,
     )
@@ -503,17 +567,19 @@
 
     for side in range(2):
         arrived(edge_in.at[side], s_edge.at[side], r_edge.at[side])
-    back = scattered(2, True)
-    adjoint_copies = []
+    back = scattered(2, None, True)
     for l in range(2):
         cols = slice(l * TILE, (l + 1) * TILE)
         added = nacc[:, cols] + edge_in[l].astype(F32) + expanded(back, sbasis, l)
         adjoint[:, cols] = adjoint[:, cols] - DAMPING * added
-        copy = pltpu.make_async_copy(
-            adjoint.at[:, cols], adj_out.at[:, cols], local_sem.at[11 + l]
-        )
-        copy.start()
-        adjoint_copies.append(copy)
+        for k in range(4):
+            copy = pltpu.make_async_copy(
+                adjoint.at[k * half : (k + 1) * half, cols],
+                adj_out.at[k % 2, (k // 2) * half : (k // 2 + 1) * half, cols],
+                local_sem.at[17 + 4 * l + k],
+            )
+            copy.start()
+            copies.append(copy)
 
     lines = (focal_count + 127) // 128
     for d in range(1, nq):
@@ -538,24 +604,23 @@
 
     for copy in pending:
         copy.wait_send()
-    field_copy.wait()
-    for copy in adjoint_copies:
+    for copy in copies:
         copy.wait()
 
 
-CHUNKS = 4
+CHUNKS = 2
 
 
 def hand_out(field, residual, adjoint, field_out, residual_out, adjoint_out, held, in_sem, out_sem):
     residual_out[...] = residual[...]
-    rows = held.shape[1] // CHUNKS
+    rows = held.shape[2] // CHUNKS
     loads, stores = [], []
     for k, (source, target) in enumerate(((field, field_out), (adjoint, adjoint_out))):
-        for c in range(CHUNKS):
-            part = pl.ds(c * rows, rows)
-            here = held.at[k, part]
-            loads.append(pltpu.make_async_copy(source.at[part], here, in_sem.at[k, c]))
-            stores.append(pltpu.make_async_copy(here, target.at[part], out_sem.at[k, c]))
+        for c in range(2 * CHUNKS):
+            part = pl.ds((c // 2) * rows, rows)
+            here = held.at[k, c % 2, part]
+            loads.append(pltpu.make_async_copy(source.at[c % 2, part], here, in_sem.at[k, c]))
+            stores.append(pltpu.make_async_copy(here, target.at[c % 2, part], out_sem.at[k, c]))
     for copy in loads:
         copy.start()
     for load, store in zip(loads, stores):
@@ -597,9 +662,9 @@
     field, residual, adjoint = pl.pallas_call(
         functools.partial(kernel, nz, nq, ns),
         out_shape=(
-            jax.ShapeDtypeStruct((both, width), F32),
+            jax.ShapeDtypeStruct((2, ROWS, width), F32),
             jax.ShapeDtypeStruct((1, 8), F32),
-            jax.ShapeDtypeStruct((both, width), F32),
+            jax.ShapeDtypeStruct((2, ROWS, width), F32),
         ),
         in_specs=[anywhere] * 10,
         out_specs=(anywhere, vmem, anywhere),
@@ -636,19 +701,19 @@
             pltpu.VMEM((nq, 8, 128), F32),
             pltpu.VMEM((2, both, TILE), BF16),
             pltpu.VMEM((2, both, TILE), BF16),
-            dma((13,)),
-            dma((2, 2)),
-            dma((2, 2)),
+            dma((25,)),
+            dma((2, 2, 2)),
+            dma((2, 2, 2)),
             dma((nq,)),
             dma((nq,)),
-            dma((3, most)),
-            dma((3, most)),
-            dma((3, most)),
-            dma((3, most)),
-            dma((nq,)),
-            dma((nq,)),
-            dma((nz,)),
-            dma((nz,)),
+            dma((3, 2, most)),
+            dma((3, 2, most)),
+            dma((3, 2, most)),
+            dma((3, 2, most)),
+            dma((2, nq)),
+            dma((2, nq)),
+            dma((2, nz)),
+            dma((2, nz)),
             dma((ns,)),
             dma((ns,)),
             dma((nq,)),
@@ -664,7 +729,7 @@
             collective_id=0, has_side_effects=True, vmem_limit_bytes=56 * 1024 * 1024
         ),
     )(
-        excitation.reshape(both, width),
+        excitation,
         near_blocks,
         source_basis.reshape(2, PAIR, TILE),
         target_basis.reshape(2, PAIR, TILE),
@@ -678,23 +743,23 @@
     field, residual, adjoint = pl.pallas_call(
         hand_out,
         out_shape=(
-            jax.ShapeDtypeStruct((both, width), F32),
+            jax.ShapeDtypeStruct((2, ROWS, width), F32),
             jax.ShapeDtypeStruct((1, 8), F32),
-            jax.ShapeDtypeStruct((both, width), F32),
+            jax.ShapeDtypeStruct((2, ROWS, width), F32),
         ),
         in_specs=[anywhere, vmem, anywhere],
         out_specs=[anywhere, vmem, anywhere],
         scratch_shapes=[
-            pltpu.VMEM((2, both, width), F32),
-            dma((2, CHUNKS)),
-            dma((2, CHUNKS)),
+            pltpu.VMEM((2, 2, ROWS, width), F32),
+            dma((2, 2 * CHUNKS)),
+            dma((2, 2 * CHUNKS)),
         ],
         compiler_params=pltpu.CompilerParams(vmem_limit_bytes=56 * 1024 * 1024),
     )(field, residual, adjoint)
     return (
-        field.reshape(2, ROWS, width),
+        field,
         residual.reshape(8),
-        adjoint.reshape(2, ROWS, width),
+        adjoint,
     )
 
 

time: 83.8 us -> 82.5 us (0.984)
  Pallas kernels: 82.5 us -> 81.3 us
    pallas_call x1, Pallas kernels: 79 us -> 77.8 us  [per_device(): pl.pallas_call(functools.partial(kernel, nz, nq, ns), out_shape=(jax.Shap...]
where the time goes in v4:
time: 82.5 us; the launch traced here: 82 us
  Pallas kernels  81.3 us (99%)
    pallas_call x1, Pallas kernels, per_device(): pl.pallas_call(functools.partial(kernel, nz, nq, ns), out_shape=(jax.Shap...  77.8 us
    pallas_call x1, Pallas kernels, per_device(): pl.pallas_call(hand_out, out_shape=(jax.ShapeDtypeStruct((2, ROWS, width)...  3.51 us

profile of v4, /device:TPU:2, one launch (start us, length us, event | category | flops | bytes accessed | tf_op | source)
XLA Modules:
  0.0 82.0 jit_solution(5379231812024591606)
XLA Ops:
  0.6 77.8 %shard_map.121 = (f32[2,128,1024]{2,1,0:T(8,128)}, f32[1,8]{1,0:T(1,128)}, f32[2,128,1024]{2,1,0:T(8,128)}) custom-call(bf16[2,128,1024]{2,1,0:T(8,128)(2,1)} %exc_hbm.1, bf16[2,3,2,512,512]{4,3,2,1,0:T(8,128)(2,1)} %near_hbm.1, bf16[2,48,512]{2,1,0:T(8,128)(2,1)} %bitcast.9, bf16[2,48,512]{2,1,0:T(8,128)(2,1)} %bitcast.10, bf16[2,48,3072]{2,1,0:T(8,128)(2,1)} %bitcast.8, ...), custom_call_target="tpu_custom_call" | custom-call | tf_op jit(solution)/shard_map/pallas_call | solution.py:662
  78.5 3.5 %shard_map.122 = (f32[2,128,1024]{2,1,0:T(8,128)}, f32[1,8]{1,0:T(1,128)}, f32[2,128,1024]{2,1,0:T(8,128)}) custom-call(f32[2,128,1024]{2,1,0:T(8,128)} %get-tuple-element.9.field, f32[1,8]{1,0:T(1,128)} %get-tuple-element.10.residual, f32[2,128,1024]{2,1,0:T(8,128)} %get-tuple-element.11.adjoint), custom_call_target="tpu_custom_call" | custom-call | tf_op jit(solution)/shard_map/pallas_call | solution.py:743

commit v5 on v4

--- a/solution.py
+++ b/solution.py
@@ -104,6 +104,8 @@
     rgath,
     edge_send,
     edge_in,
+    seen,
+    seen_own,
     local_sem,
     s_halo,
     r_halo,
@@ -121,6 +123,10 @@
     r_i,
     s_sib,
     r_sib,
+    s_seen,
+    r_seen,
+    s_pass,
+    r_pass,
     s_wg,
     r_wg,
     s_rr,
@@ -190,7 +196,8 @@
         )
     ):
         loads[name] = pltpu.make_async_copy(source, place, local_sem.at[k])
-        loads[name].start()
+        if name in ("exc", "sbasis", "rank", "link", "coup") or name[0] == "exc":
+            loads[name].start()
 
     pending = []
 
@@ -305,6 +312,7 @@
         for c in range(2):
             loads["exc", h, c].wait()
     loads["sbasis"].wait()
+    loads["near"].start()
     first_coeff = projected(vb[0], sbasis)
     loads["rank"].wait()
     loads["link"].wait()
@@ -329,12 +337,6 @@
     )
     limit_rows = jnp.concatenate(limits, axis=0).astype(BF16)
 
-    pl.semaphore_wait(barrier, count)
-
-    for h in range(2):
-        gather(0, h, first_coeff[:, half_of(h)], True)
-        send_halo(0, h)
-
     loads["coup"].wait()
     tile_row = lax.broadcasted_iota(jnp.int32, (tiles, group), 0)
     lane = lax.broadcasted_iota(jnp.int32, (tiles, group), 1)
@@ -353,14 +355,23 @@
                 mt[c, own_slice(q), :] = block
             else:
                 mt_send[d] = block
-        if d != 0:
-            send(
-                mt_send.at[d],
-                mt.at[core, own_slice(q), :],
-                s_mt.at[d],
-                r_mt.at[d],
-                tile=q_peer(d),
-            )
+
+    pl.semaphore_wait(barrier, count)
+
+    for h in range(2):
+        gather(0, h, first_coeff[:, half_of(h)], True)
+    for d in far_order(nq):
+        send(
+            mt_send.at[d],
+            mt.at[core, own_slice(q), :],
+            s_mt.at[d],
+            r_mt.at[d],
+            tile=q_peer(d),
+        )
+    for h in range(2):
+        send_halo(0, h)
+    for name in ("tbasis", "fk", "target", "owner"):
+        loads[name].start()
 
     def near_own(stage, h):
         rows = half_of(h)
@@ -439,6 +450,16 @@
         near_own(1, h)
         couple(1, h)
     loads["fk"].wait()
+    for l in range(2):
+        cols = slice(l * TILE, (l + 1) * TILE)
+        by_re = dot_nt(tbasis[l], fk[0, :, cols])
+        by_im = dot_nt(tbasis[l], fk[1, :, cols])
+        seen_own[0, l * RANK : (l + 1) * RANK] = by_re[:RANK] - by_im[RANK:]
+        seen_own[1, l * RANK : (l + 1) * RANK] = by_im[:RANK] + by_re[RANK:]
+    seen[:, own_slice(q), :] = seen_own[...].astype(BF16)
+    for d in far_order(nq):
+        here = seen.at[core, own_slice(q), :]
+        send(here, here, s_seen.at[d], r_seen.at[d], tile=q_peer(d))
     copies = []
 
     def f_rows(index):
@@ -480,6 +501,10 @@
                 r_fz.at[h, d],
                 tile=z_peer(d),
             )
+    for d in range(1, nq):
+        here = seen.at[core, own_slice(lax.rem(q + nq - d, nq)), :]
+        arrived(here, s_seen.at[d], r_seen.at[d])
+        send(here, here, s_pass.at[d], r_pass.at[d], src=sibling)
     row = lax.broadcasted_iota(jnp.int32, (fgroup, 128), 0)
     lane128 = lax.broadcasted_iota(jnp.int32, (fgroup, 128), 1)
     shift = lax.rem(q * fgroup, 128)
@@ -523,29 +548,30 @@
 
     scale = float(tiles * TILE / focal_count) ** 0.5
 
-    @pl.loop(0, 4)
-    def _(step):
-        cols = aligned(step * HALF, HALF, HALF)
+    for i in range(2):
         w = wt[...]
-        u = rows_joined(dot(w, fk[0, :, cols]), dot(w, fk[1, :, cols])) * scale
-        adjoint[:, cols] = u
-        vb[3, :, cols] = u.astype(BF16)
-
-    gather(2, None, projected(vb[3], tbasis), False)
-
-    @pl.loop(0, 4)
-    def _(step):
-        i = step // 2
-        half = aligned((step % 2) * HALF, HALF, HALF)
-        x = vb[3, :, aligned(i * TILE, TILE, TILE)]
-        by_re = dot_nt(x, near[i, 2 * i, 0, half, :])
-        by_im = dot_nt(x, near[i, 2 * i, 1, half, :])
-        edge_send[i, :, half] = rows_joined(by_re, by_im).astype(BF16)
-
-    send(edge_send.at[0], edge_in.at[1], s_edge.at[0], r_edge.at[1], tile=left)
-    send(edge_send.at[1], edge_in.at[0], s_edge.at[1], r_edge.at[0], tile=right)
-
-    coefficients = gathered(2, None, False)
+        for k in range(2):
+            cols = slice((2 * i + k) * HALF, (2 * i + k + 1) * HALF)
+            u = rows_joined(dot(w, fk[0, :, cols]), dot(w, fk[1, :, cols])) * scale
+            adjoint[:, cols] = u
+            vb[3, :, cols] = u.astype(BF16)
+        x = vb[3, :, i * TILE : (i + 1) * TILE]
+        by_re = dot_nt(x, near[i, 2 * i, 0])
+        by_im = dot_nt(x, near[i, 2 * i, 1])
+        edge_send[i] = rows_joined(by_re, by_im).astype(BF16)
+        send(
+            edge_send.at[i],
+            edge_in.at[1 - i],
+            s_edge.at[i],
+            r_edge.at[1 - i],
+            tile=right if i else left,
+        )
+
+    for d in range(1, nq):
+        here = seen.at[1 - core, own_slice(lax.rem(q + nq - d, nq)), :]
+        arrived(here, s_pass.at[d], r_pass.at[d])
+    w = wg[...]
+    coefficients = (lanes_joined(dot(seen[0], w), dot(seen[1], w)) * scale).astype(BF16)
     scatter(
         2,
         None,
@@ -701,6 +727,8 @@
             pltpu.VMEM((nq, 8, 128), F32),
             pltpu.VMEM((2, both, TILE), BF16),
             pltpu.VMEM((2, both, TILE), BF16),
+            pltpu.VMEM((2, spread, focal_count), BF16),
+            pltpu.VMEM((2, PAIR, focal_count), F32),
             dma((25,)),
             dma((2, 2, 2)),
             dma((2, 2, 2)),
@@ -716,6 +744,10 @@
             dma((2, nz)),
             dma((ns,)),
             dma((ns,)),
+            dma((nq,)),
+            dma((nq,)),
+            dma((nq,)),
+            dma((nq,)),
             dma((nq,)),
             dma((nq,)),
             dma((nq,)),

time: 82.5 us -> 83.5 us (1.012)
  Pallas kernels: 81.3 us -> 82.7 us
    pallas_call x1, Pallas kernels: 77.8 us -> 79.2 us  [per_device(): pl.pallas_call(functools.partial(kernel, nz, nq, ns), out_shape=(jax.Shap...]
where the time goes in v5:
time: 83.5 us; the launch traced here: 83.3 us
  Pallas kernels  82.7 us (99%)
    pallas_call x1, Pallas kernels, per_device(): pl.pallas_call(functools.partial(kernel, nz, nq, ns), out_shape=(jax.Shap...  79.2 us
    pallas_call x1, Pallas kernels, per_device(): pl.pallas_call(hand_out, out_shape=(jax.ShapeDtypeStruct((2, ROWS, width)...  3.51 us

profile of v5, /device:TPU:2, one launch (start us, length us, event | category | flops | bytes accessed | tf_op | source)
XLA Modules:
  0.0 83.3 jit_solution(2344983925594811141)
XLA Ops:
  0.6 79.2 %shard_map.121 = (f32[2,128,1024]{2,1,0:T(8,128)}, f32[1,8]{1,0:T(1,128)}, f32[2,128,1024]{2,1,0:T(8,128)}) custom-call(bf16[2,128,1024]{2,1,0:T(8,128)(2,1)} %exc_hbm.1, bf16[2,3,2,512,512]{4,3,2,1,0:T(8,128)(2,1)} %near_hbm.1, bf16[2,48,512]{2,1,0:T(8,128)(2,1)} %bitcast.9, bf16[2,48,512]{2,1,0:T(8,128)(2,1)} %bitcast.10, bf16[2,48,3072]{2,1,0:T(8,128)(2,1)} %bitcast.8, ...), custom_call_target="tpu_custom_call" | custom-call | tf_op jit(solution)/shard_map/pallas_call | solution.py:688
  79.8 3.5 %shard_map.122 = (f32[2,128,1024]{2,1,0:T(8,128)}, f32[1,8]{1,0:T(1,128)}, f32[2,128,1024]{2,1,0:T(8,128)}) custom-call(f32[2,128,1024]{2,1,0:T(8,128)} %get-tuple-element.9.field, f32[1,8]{1,0:T(1,128)} %get-tuple-element.10.residual, f32[2,128,1024]{2,1,0:T(8,128)} %get-tuple-element.11.adjoint), custom_call_target="tpu_custom_call" | custom-call | tf_op jit(solution)/shard_map/pallas_call | solution.py:775

commit v6 on v5

--- a/solution.py
+++ b/solution.py
@@ -133,6 +133,8 @@
     r_rr,
     s_edge,
     r_edge,
+    s_over,
+    r_over,
 ):
     t = lax.axis_index("tile")
     s = lax.axis_index("src")
@@ -457,9 +459,18 @@
         seen_own[0, l * RANK : (l + 1) * RANK] = by_re[:RANK] - by_im[RANK:]
         seen_own[1, l * RANK : (l + 1) * RANK] = by_im[:RANK] + by_re[RANK:]
     seen[:, own_slice(q), :] = seen_own[...].astype(BF16)
-    for d in far_order(nq):
-        here = seen.at[core, own_slice(q), :]
-        send(here, here, s_seen.at[d], r_seen.at[d], tile=q_peer(d))
+    flip = jnp.where(core == 0, -1.0, 1.0)
+
+    @pl.loop(0, 4)
+    def _(step):
+        i = step // 2
+        points = aligned((step % 2) * (focal_count // 2), focal_count // 2, 16)
+        cols = aligned(i * TILE, TILE, TILE)
+        edge_send[i, points, :] = (
+            dot_nt(fk[0, points, cols], near[i, 2 * i, core])
+            + flip * dot_nt(fk[1, points, cols], near[i, 2 * i, 1 - core])
+        ).astype(BF16)
+
     copies = []
 
     def f_rows(index):
@@ -501,10 +512,17 @@
                 r_fz.at[h, d],
                 tile=z_peer(d),
             )
-    for d in range(1, nq):
-        here = seen.at[core, own_slice(lax.rem(q + nq - d, nq)), :]
-        arrived(here, s_seen.at[d], r_seen.at[d])
-        send(here, here, s_pass.at[d], r_pass.at[d], src=sibling)
+    for d in far_order(nq):
+        here = seen.at[core, own_slice(q), :]
+        send(here, here, s_seen.at[d], r_seen.at[d], tile=q_peer(d))
+    for i in range(2):
+        send(
+            edge_send.at[i],
+            edge_in.at[1 - i, core],
+            s_edge.at[i],
+            r_edge.at[1 - i],
+            tile=right if i else left,
+        )
     row = lax.broadcasted_iota(jnp.int32, (fgroup, 128), 0)
     lane128 = lax.broadcasted_iota(jnp.int32, (fgroup, 128), 1)
     shift = lax.rem(q * fgroup, 128)
@@ -542,31 +560,13 @@
     for d in far_order(nq):
         send(rrow, rgath.at[q], s_rr.at[d], r_rr.at[d], tile=q_peer(d))
     for d in range(1, nq):
+        here = seen.at[core, own_slice(lax.rem(q + nq - d, nq)), :]
+        arrived(here, s_seen.at[d], r_seen.at[d])
+        send(here, here, s_pass.at[d], r_pass.at[d], src=sibling)
+    for d in range(1, nq):
         sender = lax.rem(q + nq - d, nq)
         arrived(wg.at[aligned(sender * fgroup, fgroup, 16)], s_wg.at[d], r_wg.at[d])
-    wt[...] = jnp.transpose(wg[...].astype(F32)).astype(BF16)
-
     scale = float(tiles * TILE / focal_count) ** 0.5
-
-    for i in range(2):
-        w = wt[...]
-        for k in range(2):
-            cols = slice((2 * i + k) * HALF, (2 * i + k + 1) * HALF)
-            u = rows_joined(dot(w, fk[0, :, cols]), dot(w, fk[1, :, cols])) * scale
-            adjoint[:, cols] = u
-            vb[3, :, cols] = u.astype(BF16)
-        x = vb[3, :, i * TILE : (i + 1) * TILE]
-        by_re = dot_nt(x, near[i, 2 * i, 0])
-        by_im = dot_nt(x, near[i, 2 * i, 1])
-        edge_send[i] = rows_joined(by_re, by_im).astype(BF16)
-        send(
-            edge_send.at[i],
-            edge_in.at[1 - i],
-            s_edge.at[i],
-            r_edge.at[1 - i],
-            tile=right if i else left,
-        )
-
     for d in range(1, nq):
         here = seen.at[1 - core, own_slice(lax.rem(q + nq - d, nq)), :]
         arrived(here, s_pass.at[d], r_pass.at[d])
@@ -578,6 +578,20 @@
         lanes_joined(dot(mback[0], coefficients), dot(mback[1], coefficients)),
         True,
     )
+    wt[...] = jnp.transpose(wg[...].astype(F32)).astype(BF16)
+
+    @pl.loop(0, 4)
+    def _(step):
+        cols = aligned(step * HALF, HALF, HALF)
+        w = wt[...]
+        u = rows_joined(dot(w, fk[0, :, cols]), dot(w, fk[1, :, cols])) * scale
+        adjoint[:, cols] = u
+        vb[3, :, cols] = u.astype(BF16)
+
+    for side in range(2):
+        here = edge_in.at[side, core]
+        arrived(here, s_edge.at[side], r_edge.at[side])
+        send(here, here, s_over.at[side], r_over.at[side], src=sibling)
 
     @pl.loop(0, 4)
     def _(step):
@@ -592,11 +606,21 @@
         nacc[:, aligned(step * HALF, HALF, HALF)] = rows_joined(by_re, by_im)
 
     for side in range(2):
-        arrived(edge_in.at[side], s_edge.at[side], r_edge.at[side])
+        arrived(edge_in.at[side, 1 - core], s_over.at[side], r_over.at[side])
+
+    @pl.loop(0, 4)
+    def _(step):
+        side = step // 2
+        cols = aligned((step % 2) * HALF, HALF, HALF)
+        w = wt[...]
+        edge = rows_joined(dot(w, edge_in[side, 0, :, cols]), dot(w, edge_in[side, 1, :, cols]))
+        out = aligned(step * HALF, HALF, HALF)
+        nacc[:, out] = nacc[:, out] + edge * scale
+
     back = scattered(2, None, True)
     for l in range(2):
         cols = slice(l * TILE, (l + 1) * TILE)
-        added = nacc[:, cols] + edge_in[l].astype(F32) + expanded(back, sbasis, l)
+        added = nacc[:, cols] + expanded(back, sbasis, l)
         adjoint[:, cols] = adjoint[:, cols] - DAMPING * added
         for k in range(4):
             copy = pltpu.make_async_copy(
@@ -725,8 +749,8 @@
             pltpu.VMEM((both, focal_count), BF16),
             pltpu.VMEM((8, 128), F32),
             pltpu.VMEM((nq, 8, 128), F32),
-            pltpu.VMEM((2, both, TILE), BF16),
-            pltpu.VMEM((2, both, TILE), BF16),
+            pltpu.VMEM((2, focal_count, TILE), BF16),
+            pltpu.VMEM((2, 2, focal_count, TILE), BF16),
             pltpu.VMEM((2, spread, focal_count), BF16),
             pltpu.VMEM((2, PAIR, focal_count), F32),
             dma((25,)),
@@ -754,6 +778,8 @@
             dma((nq,)),
             dma((nq,)),
             dma((nq,)),
+            dma((2,)),
+            dma((2,)),
             dma((2,)),
             dma((2,)),
         ],

time: 83.5 us -> 85.2 us (1.020)
  the two profiles are of different devices: /device:TPU:2 before, /device:TPU:1 now
where the time goes in v6:
time: 85.2 us; the launch traced here: 85.1 us
  Pallas kernels  84.4 us (99%)
    pallas_call x1, Pallas kernels, per_device(): pl.pallas_call(functools.partial(kernel, nz, nq, ns), out_shape=(jax.Shap...  80.9 us
    pallas_call x1, Pallas kernels, per_device(): pl.pallas_call(hand_out, out_shape=(jax.ShapeDtypeStruct((2, ROWS, width)...  3.51 us

profile of v6, /device:TPU:1, one launch (start us, length us, event | category | flops | bytes accessed | tf_op | source)
XLA Modules:
  0.0 85.1 jit_solution(4726888227288460448)
XLA Ops:
  0.6 80.9 %shard_map.121 = (f32[2,128,1024]{2,1,0:T(8,128)}, f32[1,8]{1,0:T(1,128)}, f32[2,128,1024]{2,1,0:T(8,128)}) custom-call(bf16[2,128,1024]{2,1,0:T(8,128)(2,1)} %exc_hbm.1, bf16[2,3,2,512,512]{4,3,2,1,0:T(8,128)(2,1)} %near_hbm.1, bf16[2,48,512]{2,1,0:T(8,128)(2,1)} %bitcast.9, bf16[2,48,512]{2,1,0:T(8,128)(2,1)} %bitcast.10, bf16[2,48,3072]{2,1,0:T(8,128)(2,1)} %bitcast.8, ...), custom_call_target="tpu_custom_call" | custom-call | tf_op jit(solution)/shard_map/pallas_call | solution.py:712
  81.5 3.5 %shard_map.122 = (f32[2,128,1024]{2,1,0:T(8,128)}, f32[1,8]{1,0:T(1,128)}, f32[2,128,1024]{2,1,0:T(8,128)}) custom-call(f32[2,128,1024]{2,1,0:T(8,128)} %get-tuple-element.9.field, f32[1,8]{1,0:T(1,128)} %get-tuple-element.10.residual, f32[2,128,1024]{2,1,0:T(8,128)} %get-tuple-element.11.adjoint), custom_call_target="tpu_custom_call" | custom-call | tf_op jit(solution)/shard_map/pallas_call | solution.py:801

commit v7 on v5

--- a/solution.py
+++ b/solution.py
@@ -360,6 +360,7 @@
 
     for h in range(2):
         gather(0, h, first_coeff[:, half_of(h)], True)
+        send_halo(0, h)
     for d in far_order(nq):
         send(
             mt_send.at[d],
@@ -368,8 +369,6 @@
             r_mt.at[d],
             tile=q_peer(d),
         )
-    for h in range(2):
-        send_halo(0, h)
     for name in ("tbasis", "fk", "target", "owner"):
         loads[name].start()
 
@@ -457,9 +456,6 @@
         seen_own[0, l * RANK : (l + 1) * RANK] = by_re[:RANK] - by_im[RANK:]
         seen_own[1, l * RANK : (l + 1) * RANK] = by_im[:RANK] + by_re[RANK:]
     seen[:, own_slice(q), :] = seen_own[...].astype(BF16)
-    for d in far_order(nq):
-        here = seen.at[core, own_slice(q), :]
-        send(here, here, s_seen.at[d], r_seen.at[d], tile=q_peer(d))
     copies = []
 
     def f_rows(index):
@@ -501,10 +497,9 @@
                 r_fz.at[h, d],
                 tile=z_peer(d),
             )
-    for d in range(1, nq):
-        here = seen.at[core, own_slice(lax.rem(q + nq - d, nq)), :]
-        arrived(here, s_seen.at[d], r_seen.at[d])
-        send(here, here, s_pass.at[d], r_pass.at[d], src=sibling)
+    for d in far_order(nq):
+        here = seen.at[core, own_slice(q), :]
+        send(here, here, s_seen.at[d], r_seen.at[d], tile=q_peer(d))
     row = lax.broadcasted_iota(jnp.int32, (fgroup, 128), 0)
     lane128 = lax.broadcasted_iota(jnp.int32, (fgroup, 128), 1)
     shift = lax.rem(q * fgroup, 128)
@@ -541,6 +536,10 @@
     rgath[q] = jnp.broadcast_to(flat, (8, 128))
     for d in far_order(nq):
         send(rrow, rgath.at[q], s_rr.at[d], r_rr.at[d], tile=q_peer(d))
+    for d in range(1, nq):
+        here = seen.at[core, own_slice(lax.rem(q + nq - d, nq)), :]
+        arrived(here, s_seen.at[d], r_seen.at[d])
+        send(here, here, s_pass.at[d], r_pass.at[d], src=sibling)
     for d in range(1, nq):
         sender = lax.rem(q + nq - d, nq)
         arrived(wg.at[aligned(sender * fgroup, fgroup, 16)], s_wg.at[d], r_wg.at[d])

time: 83.5 us -> 80.6 us (0.965)
  Pallas kernels: 82.7 us -> 79.8 us
    pallas_call x1, Pallas kernels: 79.2 us -> 76.3 us  [per_device(): pl.pallas_call(functools.partial(kernel, nz, nq, ns), out_shape=(jax.Shap...]
where the time goes in v7:
time: 80.6 us; the launch traced here: 80.4 us
  Pallas kernels  79.8 us (99%)
    pallas_call x1, Pallas kernels, per_device(): pl.pallas_call(functools.partial(kernel, nz, nq, ns), out_shape=(jax.Shap...  76.3 us
    pallas_call x1, Pallas kernels, per_device(): pl.pallas_call(hand_out, out_shape=(jax.ShapeDtypeStruct((2, ROWS, width)...  3.51 us

profile of v7, /device:TPU:2, one launch (start us, length us, event | category | flops | bytes accessed | tf_op | source)
XLA Modules:
  0.0 80.4 jit_solution(17395961125652513250)
XLA Ops:
  0.6 76.3 %shard_map.121 = (f32[2,128,1024]{2,1,0:T(8,128)}, f32[1,8]{1,0:T(1,128)}, f32[2,128,1024]{2,1,0:T(8,128)}) custom-call(bf16[2,128,1024]{2,1,0:T(8,128)(2,1)} %exc_hbm.1, bf16[2,3,2,512,512]{4,3,2,1,0:T(8,128)(2,1)} %near_hbm.1, bf16[2,48,512]{2,1,0:T(8,128)(2,1)} %bitcast.9, bf16[2,48,512]{2,1,0:T(8,128)(2,1)} %bitcast.10, bf16[2,48,3072]{2,1,0:T(8,128)(2,1)} %bitcast.8, ...), custom_call_target="tpu_custom_call" | custom-call | tf_op jit(solution)/shard_map/pallas_call | solution.py:687
  76.9 3.5 %shard_map.122 = (f32[2,128,1024]{2,1,0:T(8,128)}, f32[1,8]{1,0:T(1,128)}, f32[2,128,1024]{2,1,0:T(8,128)}) custom-call(f32[2,128,1024]{2,1,0:T(8,128)} %get-tuple-element.9.field, f32[1,8]{1,0:T(1,128)} %get-tuple-element.10.residual, f32[2,128,1024]{2,1,0:T(8,128)} %get-tuple-element.11.adjoint), custom_call_target="tpu_custom_call" | custom-call | tf_op jit(solution)/shard_map/pallas_call | solution.py:774

commit v8 on v7

--- a/solution.py
+++ b/solution.py
@@ -546,6 +546,7 @@
     wt[...] = jnp.transpose(wg[...].astype(F32)).astype(BF16)
 
     scale = float(tiles * TILE / focal_count) ** 0.5
+    settled = len(pending)
 
     for i in range(2):
         w = wt[...]
@@ -590,6 +591,8 @@
             by_im = by_im + dot_nt(x, near[i, m - i + 1, 1, half, :])
         nacc[:, aligned(step * HALF, HALF, HALF)] = rows_joined(by_re, by_im)
 
+    for copy in pending[:settled]:
+        copy.wait_send()
     for side in range(2):
         arrived(edge_in.at[side], s_edge.at[side], r_edge.at[side])
     back = scattered(2, None, True)
@@ -627,7 +630,7 @@
     line = jnp.sum(jnp.where(diagonal, column, 0.0), axis=0, keepdims=True)
     res_out[...] = line[:, :8]
 
-    for copy in pending:
+    for copy in pending[settled:]:
         copy.wait_send()
     for copy in copies:
         copy.wait()

time: 80.6 us -> 80.6 us (level)
  no operation moved by 1% of the time
where the time goes in v8:
time: 80.6 us; the launch traced here: 80.4 us
  Pallas kernels  79.8 us (99%)
    pallas_call x1, Pallas kernels, per_device(): pl.pallas_call(functools.partial(kernel, nz, nq, ns), out_shape=(jax.Shap...  76.3 us
    pallas_call x1, Pallas kernels, per_device(): pl.pallas_call(hand_out, out_shape=(jax.ShapeDtypeStruct((2, ROWS, width)...  3.51 us

profile of v8, /device:TPU:2, one launch (start us, length us, event | category | flops | bytes accessed | tf_op | source)
XLA Modules:
  0.0 80.4 jit_solution(15223985842098256903)
XLA Ops:
  0.6 76.3 %shard_map.121 = (f32[2,128,1024]{2,1,0:T(8,128)}, f32[1,8]{1,0:T(1,128)}, f32[2,128,1024]{2,1,0:T(8,128)}) custom-call(bf16[2,128,1024]{2,1,0:T(8,128)(2,1)} %exc_hbm.1, bf16[2,3,2,512,512]{4,3,2,1,0:T(8,128)(2,1)} %near_hbm.1, bf16[2,48,512]{2,1,0:T(8,128)(2,1)} %bitcast.9, bf16[2,48,512]{2,1,0:T(8,128)(2,1)} %bitcast.10, bf16[2,48,3072]{2,1,0:T(8,128)(2,1)} %bitcast.8, ...), custom_call_target="tpu_custom_call" | custom-call | tf_op jit(solution)/shard_map/pallas_call | solution.py:690
  76.9 3.5 %shard_map.122 = (f32[2,128,1024]{2,1,0:T(8,128)}, f32[1,8]{1,0:T(1,128)}, f32[2,128,1024]{2,1,0:T(8,128)}) custom-call(f32[2,128,1024]{2,1,0:T(8,128)} %get-tuple-element.9.field, f32[1,8]{1,0:T(1,128)} %get-tuple-element.10.residual, f32[2,128,1024]{2,1,0:T(8,128)} %get-tuple-element.11.adjoint), custom_call_target="tpu_custom_call" | custom-call | tf_op jit(solution)/shard_map/pallas_call | solution.py:777
